TPU v7x, 512 devices: a whole 4x8x8 slice. The times are simulated.
512 devices in a mesh: dp: 16 (over x, y_hi), section: 4 (over y_lo, core), tensor: 8 (over z).
Axes of the slice: x: 4, y: 8 (y_hi: 4, y_lo: 2; y = y_hi * 2 + y_lo), z: 8, core: 2. Of those that a mesh axis runs over, the one named last changes fastest.
Arguments:
- latents: bfloat16 [640, 32, 256], P('tensor', 'dp'), may hold values from -40 to 40
- target: bfloat16 [640, 32, 256], P('tensor', 'dp'), may hold values from -6 to 6
- base_weight: bfloat16 [4, 640, 9, 640], P('section', 'tensor'), may hold values from -0.078125 to 0.078125
- seeds: int32 [4], P('section'), may hold values from 0 to 65520
- timesteps: int32 [32], P('dp'), may hold values from 0 to 999
- time_table: bfloat16 [4, 1000, 640], P('section', None, 'tensor'), may hold values from -4 to 4
Outputs:
- weight_grad: float32 [4, 640, 9, 640], P('section', 'tensor')
All inputs are finite; a program needn't handle non-finite values.
Results may differ from a plain program's by a relative error of at most 0.006.
Values may be sent and summed in bfloat16 or wider, within the bound.
A program may use at most 64 MiB of HBM per device.

v0:
```python
import jax
import jax.numpy as jnp
from jax import lax
from jax.sharding import PartitionSpec as P

C = 640
GROUPS = 32
RES = 16


noise_scale = 0.02


def passed_along(value, axis, steps):
    count = lax.axis_size(axis)
    first, last = (max(0, -steps), min(count, count - steps))
    return lax.ppermute(value, axis, [(source, source + steps) for source in range(first, last)])


def noise(seed_value, first_row, row_count, col_count):
    shape_all = (row_count, 9, col_count)
    channel = lax.broadcasted_iota(jnp.int32, shape_all, 0) + first_row
    kernel_tap = lax.broadcasted_iota(jnp.int32, shape_all, 1)
    out_channel = lax.broadcasted_iota(jnp.int32, shape_all, 2)
    flat_index = (channel * 9 + kernel_tap) * col_count + out_channel
    low_part = flat_index % 65521
    high_part = flat_index // 65521
    hashed = (low_part * 32749 + high_part * 12345 + seed_value) % 65521
    return hashed.astype(jnp.float32) / 65521.0 - 0.5


def activate(inputs, bias_vec, group_size):
    shifted = inputs + bias_vec[:, None]
    channels = shifted.shape[0]
    pixels = shifted.shape[1]
    grouped = shifted.reshape(channels // group_size, group_size * pixels)
    center = grouped - jnp.mean(grouped, axis=1, keepdims=True)
    normed = center * lax.rsqrt(jnp.mean(center * center, axis=1, keepdims=True) + 1e-05)
    return jax.nn.silu(normed.reshape(channels, pixels))


def unfold(activation, side_len):
    channels = activation.shape[0]
    image_grid = activation.reshape(channels, side_len, side_len)
    padded = jnp.pad(image_grid, ((0, 0), (1, 1), (1, 1)))
    tap_list = [
        padded[:, shift_row : shift_row + side_len, shift_col : shift_col + side_len]
        for shift_row in range(3)
        for shift_col in range(3)
    ]
    return jnp.stack(tap_list, axis=1).reshape(channels, 9, side_len * side_len)


def fold_back(columns, side_len):
    channels = columns.shape[0]
    tap_parts = columns.reshape(channels, 9, side_len, side_len)
    padded = jnp.zeros((channels, side_len + 2, side_len + 2), jnp.float32)
    for shift_row in range(3):
        for shift_col in range(3):
            padded = padded.at[
                :, shift_row : shift_row + side_len, shift_col : shift_col + side_len
            ].add(tap_parts[:, shift_row * 3 + shift_col])
    return padded[:, 1:-1, 1:-1].reshape(channels, side_len * side_len)


def body(latents, target, base_weight, seeds, timesteps, time_table):
    section_count = lax.axis_size("section")
    section_index = lax.axis_index("section")
    tensor_index = lax.axis_index("tensor")
    local_in = base_weight.shape[1]
    channel_total = base_weight.shape[3]
    latent_count = latents.shape[1]
    pixels = latents.shape[2]
    side_len = RES
    group_size = C // GROUPS
    total_latents = latent_count * lax.axis_size("dp")
    last_section = section_count - 1
    tick_total = latent_count + section_count - 1
    weight_local = (
        base_weight[0].astype(jnp.float32)
        + noise_scale * noise(seeds[0], tensor_index * local_in, local_in, channel_total)
    ).astype(jnp.bfloat16)
    steps_table = time_table[0]

    def lookup(step_value):
        onehot = (jnp.arange(steps_table.shape[0], dtype=jnp.int32) == step_value).astype(
            jnp.bfloat16
        )
        return jnp.dot(onehot[None, :], steps_table, preferred_element_type=jnp.float32)[0]

    def forward_tick(tick_index, loop_state):
        incoming, saved_inputs, saved_grads = loop_state
        micro_index = tick_index - section_index
        is_valid = (micro_index >= 0) & (micro_index < latent_count)
        slot_index = jnp.clip(micro_index, 0, latent_count - 1)
        own_input = lax.dynamic_index_in_dim(latents, slot_index, 1, keepdims=False)
        section_input = jnp.where(section_index == 0, own_input, incoming)
        step_bias = lookup(timesteps[slot_index])
        inputs = section_input.astype(jnp.float32)
        activation = activate(inputs, step_bias, group_size).astype(jnp.bfloat16)
        columns = unfold(activation, side_len)
        conv_sum = lax.psum_scatter(
            lax.dot_general(
                weight_local,
                columns,
                (((0, 1), (0, 1)), ((), ())),
                preferred_element_type=jnp.float32,
            ).astype(jnp.bfloat16),
            "tensor",
            scatter_dimension=0,
            tiled=True,
        ).astype(jnp.float32)
        output = (inputs + step_bias[:, None] + conv_sum).astype(jnp.bfloat16)
        old_input = lax.dynamic_index_in_dim(saved_inputs, slot_index, 0, keepdims=False)
        saved_inputs = lax.dynamic_update_index_in_dim(
            saved_inputs, jnp.where(is_valid, section_input, old_input), slot_index, 0
        )
        target_now = lax.dynamic_index_in_dim(target, slot_index, 1, keepdims=False)
        pred_grad = (
            (output.astype(jnp.float32) - target_now.astype(jnp.float32)) / total_latents
        ).astype(jnp.bfloat16)
        keep_grad = is_valid & (section_index == last_section)
        old_grad = lax.dynamic_index_in_dim(saved_grads, slot_index, 0, keepdims=False)
        saved_grads = lax.dynamic_update_index_in_dim(
            saved_grads, jnp.where(keep_grad, pred_grad, old_grad), slot_index, 0
        )
        incoming = passed_along(output, "section", 1)
        return (incoming, saved_inputs, saved_grads)

    empty_act = jnp.zeros((local_in, pixels), jnp.bfloat16)
    empty_store = jnp.zeros((latent_count, local_in, pixels), jnp.bfloat16)
    incoming, saved_inputs, saved_grads = lax.fori_loop(
        0, tick_total, forward_tick, (empty_act, empty_store, empty_store)
    )

    def backward_tick(tick_index, loop_state):
        incoming, grad_total = loop_state
        micro_index = tick_index - (last_section - section_index)
        is_valid = (micro_index >= 0) & (micro_index < latent_count)
        slot_index = jnp.clip(micro_index, 0, latent_count - 1)
        from_last = lax.dynamic_index_in_dim(saved_grads, slot_index, 0, keepdims=False)
        out_grad = jnp.where(section_index == last_section, from_last, incoming)
        out_grad = jnp.where(is_valid, out_grad, jnp.zeros_like(out_grad))
        section_input = lax.dynamic_index_in_dim(saved_inputs, slot_index, 0, keepdims=False)
        step_bias = lookup(timesteps[slot_index])
        act_value, act_back = jax.vjp(
            lambda values: activate(values, step_bias, group_size),
            section_input.astype(jnp.float32),
        )
        columns = unfold(act_value.astype(jnp.bfloat16), side_len)
        shard_piece = lax.all_gather(out_grad, "tensor", axis=0, tiled=True)
        spread = lax.dot_general(
            weight_local, shard_piece, (((2,), (0,)), ((), ())), preferred_element_type=jnp.float32
        )
        current = (jnp.zeros((local_in, 9, pixels), jnp.float32), grad_total)[1]
        update = current + lax.dot_general(
            columns, shard_piece, (((2,), (1,)), ((), ())), preferred_element_type=jnp.float32
        )
        input_grad = act_back(fold_back(spread, side_len))[0]
        sent_grad = (out_grad.astype(jnp.float32) + input_grad).astype(jnp.bfloat16)
        incoming = passed_along(sent_grad, "section", -1)
        return (incoming, update)

    start_grad = jnp.zeros((local_in, 9, channel_total), jnp.float32)
    incoming, grad_total = lax.fori_loop(0, tick_total, backward_tick, (empty_act, start_grad))
    grad_sum = lax.psum(grad_total, "dp")
    return grad_sum[None]


def solution(mesh):
    in_specs = (
        P("tensor", "dp", None),
        P("tensor", "dp", None),
        P("section", "tensor", None, None),
        P("section"),
        P("dp"),
        P("section", None, "tensor"),
    )
    out_specs = P("section", "tensor", None, None)
    return jax.shard_map(body, mesh=mesh, in_specs=in_specs, out_specs=out_specs, check_vma=False)
```

profile of v0, /device:TPU:1, one launch (start us, length us, event | category | flops | bytes accessed | tf_op | source)
XLA Modules:
  0.0 764.1 jit_solution(11001439166971174273)
XLA Ops:
  9.9 1.8 copy.35
  11.6 4.6 fusion.50
  16.9 261.3 %while.48 = (s32[]{:T(128)}, bf16[80,256]{1,0:T(8,128)(2,1)S(1)}, bf16[2,80,256]{2,1,0:T(8,128)(2,1)S(1)}, bf16[2,80,256]{2,1,0:T(8,128)(2,1)}, pred[]{:T(512)},...) while((s32[]{:T(128)}, bf16[80,256]{1,0:T(8,128)(2,1)S(1)}, ...), condition=%wide.region_6.7_spmd, body=%wide.region_0.6_spmd.sunk | while | flops 237053168 | bytes 5682156 | solution.py:132
  24.0 40.4 %reduce-scatter.2.cloned.1.call-done = bf16[80,256]{1,0:T(8,128)(2,1)} async-done(((bf16[640,256]{1,0:T(8,128)(2,1)}), bf16[80,256]{1,0:T(8,128)(2,1)}) %reduce-scatter.2.cloned.1.call-update) | async-done | bytes 40976 | tf_op jit(solution)/shard_map/while/body/eval_jaxpr/reduce_scatter | solution.py:102
  65.9 8.4 %collective-permute-start = (bf16[80,256]{1,0:T(8,128)(2,1)S(1)}, bf16[80,256]{1,0:T(8,128)(2,1)S(1)}, u32[]{:S(2)}, u32[]{:S(2)}) collective-permute-start(bf16[80,256]{1,0:T(8,128)(2,1)S(1)} %get-tuple-element.1133), channel_id=1, source_target_pairs={{0,8},{8,16},{16,24},{1,9},{9,17},{17,25},{2,10},{10,18},{18,26},{... | collective-permute-start | bytes 122888 | tf_op jit(solution)/shard_map/while/body/eval_jaxpr/ppermute | solution.py:17
  82.4 32.7 %reduce-scatter.2.cloned.1.call-done = bf16[80,256]{1,0:T(8,128)(2,1)} async-done(((bf16[640,256]{1,0:T(8,128)(2,1)}), bf16[80,256]{1,0:T(8,128)(2,1)}) %reduce-scatter.2.cloned.1.call-update) | async-done | bytes 40976 | tf_op jit(solution)/shard_map/while/body/eval_jaxpr/reduce_scatter | solution.py:102
  116.5 8.5 %collective-permute-start = (bf16[80,256]{1,0:T(8,128)(2,1)S(1)}, bf16[80,256]{1,0:T(8,128)(2,1)S(1)}, u32[]{:S(2)}, u32[]{:S(2)}) collective-permute-start(bf16[80,256]{1,0:T(8,128)(2,1)S(1)} %get-tuple-element.1133), channel_id=1, source_target_pairs={{0,8},{8,16},{16,24},{1,9},{9,17},{17,25},{2,10},{10,18},{18,26},{... | collective-permute-start | bytes 122888 | tf_op jit(solution)/shard_map/while/body/eval_jaxpr/ppermute | solution.py:17
  133.1 32.4 %reduce-scatter.2.cloned.1.call-done = bf16[80,256]{1,0:T(8,128)(2,1)} async-done(((bf16[640,256]{1,0:T(8,128)(2,1)}), bf16[80,256]{1,0:T(8,128)(2,1)}) %reduce-scatter.2.cloned.1.call-update) | async-done | bytes 40976 | tf_op jit(solution)/shard_map/while/body/eval_jaxpr/reduce_scatter | solution.py:102
  166.9 8.8 %collective-permute-start = (bf16[80,256]{1,0:T(8,128)(2,1)S(1)}, bf16[80,256]{1,0:T(8,128)(2,1)S(1)}, u32[]{:S(2)}, u32[]{:S(2)}) collective-permute-start(bf16[80,256]{1,0:T(8,128)(2,1)S(1)} %get-tuple-element.1133), channel_id=1, source_target_pairs={{0,8},{8,16},{16,24},{1,9},{9,17},{17,25},{2,10},{10,18},{18,26},{... | collective-permute-start | bytes 122888 | tf_op jit(solution)/shard_map/while/body/eval_jaxpr/ppermute | solution.py:17
  183.8 32.6 %reduce-scatter.2.cloned.1.call-done = bf16[80,256]{1,0:T(8,128)(2,1)} async-done(((bf16[640,256]{1,0:T(8,128)(2,1)}), bf16[80,256]{1,0:T(8,128)(2,1)}) %reduce-scatter.2.cloned.1.call-update) | async-done | bytes 40976 | tf_op jit(solution)/shard_map/while/body/eval_jaxpr/reduce_scatter | solution.py:102
  218.0 8.5 %collective-permute-start = (bf16[80,256]{1,0:T(8,128)(2,1)S(1)}, bf16[80,256]{1,0:T(8,128)(2,1)S(1)}, u32[]{:S(2)}, u32[]{:S(2)}) collective-permute-start(bf16[80,256]{1,0:T(8,128)(2,1)S(1)} %get-tuple-element.1133), channel_id=1, source_target_pairs={{0,8},{8,16},{16,24},{1,9},{9,17},{17,25},{2,10},{10,18},{18,26},{... | collective-permute-start | bytes 122888 | tf_op jit(solution)/shard_map/while/body/eval_jaxpr/ppermute | solution.py:17
  234.5 32.7 %reduce-scatter.2.cloned.1.call-done = bf16[80,256]{1,0:T(8,128)(2,1)} async-done(((bf16[640,256]{1,0:T(8,128)(2,1)}), bf16[80,256]{1,0:T(8,128)(2,1)}) %reduce-scatter.2.cloned.1.call-update) | async-done | bytes 40976 | tf_op jit(solution)/shard_map/while/body/eval_jaxpr/reduce_scatter | solution.py:102
  268.7 8.4 %collective-permute-start = (bf16[80,256]{1,0:T(8,128)(2,1)S(1)}, bf16[80,256]{1,0:T(8,128)(2,1)S(1)}, u32[]{:S(2)}, u32[]{:S(2)}) collective-permute-start(bf16[80,256]{1,0:T(8,128)(2,1)S(1)} %get-tuple-element.1133), channel_id=1, source_target_pairs={{0,8},{8,16},{16,24},{1,9},{9,17},{17,25},{2,10},{10,18},{18,26},{... | collective-permute-start | bytes 122888 | tf_op jit(solution)/shard_map/while/body/eval_jaxpr/ppermute | solution.py:17
  278.8 299.7 %while.49 = (s32[]{:T(128)}, bf16[80,256]{1,0:T(8,128)(2,1)}, f32[80,9,640]{2,0,1:T(8,128)}, s32[]{:T(128)}, pred[]{:T(512)}, /*index=5*/bf16[2,80,256]{2,1,0:T(...) while((s32[]{:T(128)}, bf16[80,256]{1,0:T(8,128)(2,1)}, ...), condition=%wide.region_17.18_spmd.clone, body=%wide.region_7.17_spmd.clone.sunk | while | flops 474662176 | bytes 30336436 | solution.py:165
  285.1 18.9 %all_gather.15 = bf16[640,256]{1,0:T(8,128)(2,1)S(1)} all-gather(bf16[80,256]{1,0:T(8,128)(2,1)S(1)} %fusion.106), channel_id=1, replica_groups=mesh['dp'=16,'section'=4,'tensor'=8] {'tensor'}, dimensions={0}, use_global_device_ids=true | all-gather | bytes 368640 | tf_op jit(solution)/shard_map/while/body/eval_jaxpr/all_gather | solution.py:151
  308.4 1.9 add_select_fusion.5
  319.0 6.2 collective-permute-start.1
  344.2 19.3 %all_gather.15 = bf16[640,256]{1,0:T(8,128)(2,1)S(1)} all-gather(bf16[80,256]{1,0:T(8,128)(2,1)S(1)} %fusion.106), channel_id=1, replica_groups=mesh['dp'=16,'section'=4,'tensor'=8] {'tensor'}, dimensions={0}, use_global_device_ids=true | all-gather | bytes 368640 | tf_op jit(solution)/shard_map/while/body/eval_jaxpr/all_gather | solution.py:151
  367.9 1.9 add_select_fusion.5
  378.4 6.9 collective-permute-start.1
  404.3 19.2 %all_gather.15 = bf16[640,256]{1,0:T(8,128)(2,1)S(1)} all-gather(bf16[80,256]{1,0:T(8,128)(2,1)S(1)} %fusion.106), channel_id=1, replica_groups=mesh['dp'=16,'section'=4,'tensor'=8] {'tensor'}, dimensions={0}, use_global_device_ids=true | all-gather | bytes 368640 | tf_op jit(solution)/shard_map/while/body/eval_jaxpr/all_gather | solution.py:151
  427.9 1.9 add_select_fusion.5
  438.5 7.0 collective-permute-start.1
  464.5 19.2 %all_gather.15 = bf16[640,256]{1,0:T(8,128)(2,1)S(1)} all-gather(bf16[80,256]{1,0:T(8,128)(2,1)S(1)} %fusion.106), channel_id=1, replica_groups=mesh['dp'=16,'section'=4,'tensor'=8] {'tensor'}, dimensions={0}, use_global_device_ids=true | all-gather | bytes 368640 | tf_op jit(solution)/shard_map/while/body/eval_jaxpr/all_gather | solution.py:151
  488.1 1.9 add_select_fusion.5
  496.9 1.7 fusion.118
  498.6 7.1 collective-permute-start.1
  524.7 19.2 %all_gather.15 = bf16[640,256]{1,0:T(8,128)(2,1)S(1)} all-gather(bf16[80,256]{1,0:T(8,128)(2,1)S(1)} %fusion.106), channel_id=1, replica_groups=mesh['dp'=16,'section'=4,'tensor'=8] {'tensor'}, dimensions={0}, use_global_device_ids=true | all-gather | bytes 368640 | tf_op jit(solution)/shard_map/while/body/eval_jaxpr/all_gather | solution.py:151
  548.3 1.9 add_select_fusion.5
  558.8 7.0 collective-permute-start.1
  578.5 175.6 %all-reduce.5.cloned.1.call-done = f32[1,80,9,640]{3,1,2,0:T(8,128)} async-done(((f32[1,80,9,640]{3,1,2,0:T(8,128)}), f32[1,80,9,640]{3,1,2,0:T(8,128)}) %all-reduce.5.cloned.1.call-update) | async-done | bytes 1843216 | tf_op jit(solution)/shard_map/psum | solution.py:166
  754.1 2.9 copy.131
  (648 shorter events, 206.7 us)
Async XLA Ops:
  7.4 9.5 %copy-start.4 = (s32[2]{0:T(128)S(1)}, s32[2]{0:T(128)}, u32[]{:S(2)}) copy-start(s32[2]{0:T(128)} %param.32) | copy-start | bytes 28
  16.9 261.9 %copy-start.3 = (s32[3]{0:T(128)S(1)}, s32[3]{0:T(128)}, u32[]{:S(2)}) copy-start(s32[3]{0:T(128)} %constant.746.clone.2) | copy-start | bytes 40
  16.9 47.5 %reduce-scatter.2.cloned.1.call-start = ((), (), s32[]{:S(2)}) async-start(), calls=%async_computation.2 | async-start | bytes 368640 | tf_op jit(solution)/shard_map/while/body/eval_jaxpr/reduce_scatter | solution.py:102
  65.9 9.5 %collective-permute-start = (bf16[80,256]{1,0:T(8,128)(2,1)S(1)}, bf16[80,256]{1,0:T(8,128)(2,1)S(1)}, u32[]{:S(2)}, u32[]{:S(2)}) collective-permute-start(bf16[80,256]{1,0:T(8,128)(2,1)S(1)} %get-tuple-element.1133), channel_id=1, source_target_pairs={{0,8},{8,16},{16,24},{1,9},{9,17},{17,25},{2,10},{10,18},{18,26},{... | collective-permute-start | bytes 122888 | tf_op jit(solution)/shard_map/while/body/eval_jaxpr/ppermute | solution.py:17
  75.4 39.7 %reduce-scatter.2.cloned.1.call-start = ((), (), s32[]{:S(2)}) async-start(), calls=%async_computation.2 | async-start | bytes 368640 | tf_op jit(solution)/shard_map/while/body/eval_jaxpr/reduce_scatter | solution.py:102
  116.5 9.5 %collective-permute-start = (bf16[80,256]{1,0:T(8,128)(2,1)S(1)}, bf16[80,256]{1,0:T(8,128)(2,1)S(1)}, u32[]{:S(2)}, u32[]{:S(2)}) collective-permute-start(bf16[80,256]{1,0:T(8,128)(2,1)S(1)} %get-tuple-element.1133), channel_id=1, source_target_pairs={{0,8},{8,16},{16,24},{1,9},{9,17},{17,25},{2,10},{10,18},{18,26},{... | collective-permute-start | bytes 122888 | tf_op jit(solution)/shard_map/while/body/eval_jaxpr/ppermute | solution.py:17
  126.1 39.4 %reduce-scatter.2.cloned.1.call-start = ((), (), s32[]{:S(2)}) async-start(), calls=%async_computation.2 | async-start | bytes 368640 | tf_op jit(solution)/shard_map/while/body/eval_jaxpr/reduce_scatter | solution.py:102
  166.9 9.9 %collective-permute-start = (bf16[80,256]{1,0:T(8,128)(2,1)S(1)}, bf16[80,256]{1,0:T(8,128)(2,1)S(1)}, u32[]{:S(2)}, u32[]{:S(2)}) collective-permute-start(bf16[80,256]{1,0:T(8,128)(2,1)S(1)} %get-tuple-element.1133), channel_id=1, source_target_pairs={{0,8},{8,16},{16,24},{1,9},{9,17},{17,25},{2,10},{10,18},{18,26},{... | collective-permute-start | bytes 122888 | tf_op jit(solution)/shard_map/while/body/eval_jaxpr/ppermute | solution.py:17
  176.8 39.6 %reduce-scatter.2.cloned.1.call-start = ((), (), s32[]{:S(2)}) async-start(), calls=%async_computation.2 | async-start | bytes 368640 | tf_op jit(solution)/shard_map/while/body/eval_jaxpr/reduce_scatter | solution.py:102
  218.0 9.6 %collective-permute-start = (bf16[80,256]{1,0:T(8,128)(2,1)S(1)}, bf16[80,256]{1,0:T(8,128)(2,1)S(1)}, u32[]{:S(2)}, u32[]{:S(2)}) collective-permute-start(bf16[80,256]{1,0:T(8,128)(2,1)S(1)} %get-tuple-element.1133), channel_id=1, source_target_pairs={{0,8},{8,16},{16,24},{1,9},{9,17},{17,25},{2,10},{10,18},{18,26},{... | collective-permute-start | bytes 122888 | tf_op jit(solution)/shard_map/while/body/eval_jaxpr/ppermute | solution.py:17
  227.5 39.7 %reduce-scatter.2.cloned.1.call-start = ((), (), s32[]{:S(2)}) async-start(), calls=%async_computation.2 | async-start | bytes 368640 | tf_op jit(solution)/shard_map/while/body/eval_jaxpr/reduce_scatter | solution.py:102
  268.7 9.5 %collective-permute-start = (bf16[80,256]{1,0:T(8,128)(2,1)S(1)}, bf16[80,256]{1,0:T(8,128)(2,1)S(1)}, u32[]{:S(2)}, u32[]{:S(2)}) collective-permute-start(bf16[80,256]{1,0:T(8,128)(2,1)S(1)} %get-tuple-element.1133), channel_id=1, source_target_pairs={{0,8},{8,16},{16,24},{1,9},{9,17},{17,25},{2,10},{10,18},{18,26},{... | collective-permute-start | bytes 122888 | tf_op jit(solution)/shard_map/while/body/eval_jaxpr/ppermute | solution.py:17
  278.2 475.9 %all-reduce.5.cloned.1.call-start = ((), (), s32[]{:S(2)}) async-start(), calls=%async_computation.1 | async-start | bytes 3686400 | tf_op jit(solution)/shard_map/psum | solution.py:166
  285.1 18.9 %copy-start.2 = (bf16[80,256]{1,0:T(8,128)(2,1)}, bf16[80,256]{1,0:T(8,128)(2,1)S(1)}, u32[]{:S(2)}) copy-start(bf16[80,256]{1,0:T(8,128)(2,1)S(1)} %fusion.106) | copy-start | bytes 122884 | tf_op jit(solution)/shard_map/while
  312.9 22.9 %copy-start = (f32[80,9,640]{2,0,1:T(8,128)S(1)}, f32[80,9,640]{2,0,1:T(8,128)}, u32[]{:S(2)}) copy-start(f32[80,9,640]{2,0,1:T(8,128)} %get-tuple-element.1226) | copy-start | bytes 5529604 | tf_op jit(solution)/shard_map/while
  319.0 17.6 %collective-permute-start.1 = (bf16[80,256]{1,0:T(8,128)(2,1)}, bf16[80,256]{1,0:T(8,128)(2,1)}, u32[]{:S(2)}, u32[]{:S(2)}) collective-permute-start(bf16[80,256]{1,0:T(8,128)(2,1)} %fusion.118), channel_id=1, source_target_pairs={{8,0},{16,8},{24,16},{9,1},{17,9},{25,17},{10,2},{18,10},{26,18},{... | collective-permute-start | bytes 122888 | tf_op jit(solution)/shard_map/while/body/eval_jaxpr/ppermute | solution.py:17
  336.6 1.2 copy-start.1
  344.2 19.3 %copy-start.2 = (bf16[80,256]{1,0:T(8,128)(2,1)}, bf16[80,256]{1,0:T(8,128)(2,1)S(1)}, u32[]{:S(2)}) copy-start(bf16[80,256]{1,0:T(8,128)(2,1)S(1)} %fusion.106) | copy-start | bytes 122884 | tf_op jit(solution)/shard_map/while
  372.4 23.6 %copy-start = (f32[80,9,640]{2,0,1:T(8,128)S(1)}, f32[80,9,640]{2,0,1:T(8,128)}, u32[]{:S(2)}) copy-start(f32[80,9,640]{2,0,1:T(8,128)} %get-tuple-element.1226) | copy-start | bytes 5529604 | tf_op jit(solution)/shard_map/while
  378.4 18.4 %collective-permute-start.1 = (bf16[80,256]{1,0:T(8,128)(2,1)}, bf16[80,256]{1,0:T(8,128)(2,1)}, u32[]{:S(2)}, u32[]{:S(2)}) collective-permute-start(bf16[80,256]{1,0:T(8,128)(2,1)} %fusion.118), channel_id=1, source_target_pairs={{8,0},{16,8},{24,16},{9,1},{17,9},{25,17},{10,2},{18,10},{26,18},{... | collective-permute-start | bytes 122888 | tf_op jit(solution)/shard_map/while/body/eval_jaxpr/ppermute | solution.py:17
  396.8 1.2 copy-start.1
  404.3 19.2 %copy-start.2 = (bf16[80,256]{1,0:T(8,128)(2,1)}, bf16[80,256]{1,0:T(8,128)(2,1)S(1)}, u32[]{:S(2)}) copy-start(bf16[80,256]{1,0:T(8,128)(2,1)S(1)} %fusion.106) | copy-start | bytes 122884 | tf_op jit(solution)/shard_map/while
  432.4 23.7 %copy-start = (f32[80,9,640]{2,0,1:T(8,128)S(1)}, f32[80,9,640]{2,0,1:T(8,128)}, u32[]{:S(2)}) copy-start(f32[80,9,640]{2,0,1:T(8,128)} %get-tuple-element.1226) | copy-start | bytes 5529604 | tf_op jit(solution)/shard_map/while
  438.5 18.4 %collective-permute-start.1 = (bf16[80,256]{1,0:T(8,128)(2,1)}, bf16[80,256]{1,0:T(8,128)(2,1)}, u32[]{:S(2)}, u32[]{:S(2)}) collective-permute-start(bf16[80,256]{1,0:T(8,128)(2,1)} %fusion.118), channel_id=1, source_target_pairs={{8,0},{16,8},{24,16},{9,1},{17,9},{25,17},{10,2},{18,10},{26,18},{... | collective-permute-start | bytes 122888 | tf_op jit(solution)/shard_map/while/body/eval_jaxpr/ppermute | solution.py:17
  456.9 1.2 copy-start.1
  464.5 19.2 %copy-start.2 = (bf16[80,256]{1,0:T(8,128)(2,1)}, bf16[80,256]{1,0:T(8,128)(2,1)S(1)}, u32[]{:S(2)}) copy-start(bf16[80,256]{1,0:T(8,128)(2,1)S(1)} %fusion.106) | copy-start | bytes 122884 | tf_op jit(solution)/shard_map/while
  492.5 23.8 %copy-start = (f32[80,9,640]{2,0,1:T(8,128)S(1)}, f32[80,9,640]{2,0,1:T(8,128)}, u32[]{:S(2)}) copy-start(f32[80,9,640]{2,0,1:T(8,128)} %get-tuple-element.1226) | copy-start | bytes 5529604 | tf_op jit(solution)/shard_map/while
  498.6 18.5 %collective-permute-start.1 = (bf16[80,256]{1,0:T(8,128)(2,1)}, bf16[80,256]{1,0:T(8,128)(2,1)}, u32[]{:S(2)}, u32[]{:S(2)}) collective-permute-start(bf16[80,256]{1,0:T(8,128)(2,1)} %fusion.118), channel_id=1, source_target_pairs={{8,0},{16,8},{24,16},{9,1},{17,9},{25,17},{10,2},{18,10},{26,18},{... | collective-permute-start | bytes 122888 | tf_op jit(solution)/shard_map/while/body/eval_jaxpr/ppermute | solution.py:17
  517.1 1.2 copy-start.1
  524.7 19.2 %copy-start.2 = (bf16[80,256]{1,0:T(8,128)(2,1)}, bf16[80,256]{1,0:T(8,128)(2,1)S(1)}, u32[]{:S(2)}) copy-start(bf16[80,256]{1,0:T(8,128)(2,1)S(1)} %fusion.106) | copy-start | bytes 122884 | tf_op jit(solution)/shard_map/while
  552.8 23.7 %copy-start = (f32[80,9,640]{2,0,1:T(8,128)S(1)}, f32[80,9,640]{2,0,1:T(8,128)}, u32[]{:S(2)}) copy-start(f32[80,9,640]{2,0,1:T(8,128)} %get-tuple-element.1226) | copy-start | bytes 5529604 | tf_op jit(solution)/shard_map/while
  558.8 18.4 %collective-permute-start.1 = (bf16[80,256]{1,0:T(8,128)(2,1)}, bf16[80,256]{1,0:T(8,128)(2,1)}, u32[]{:S(2)}, u32[]{:S(2)}) collective-permute-start(bf16[80,256]{1,0:T(8,128)(2,1)} %fusion.118), channel_id=1, source_target_pairs={{8,0},{16,8},{24,16},{9,1},{17,9},{25,17},{10,2},{18,10},{26,18},{... | collective-permute-start | bytes 122888 | tf_op jit(solution)/shard_map/while/body/eval_jaxpr/ppermute | solution.py:17
  (1 other events, 1.2 us)
Sparse Core Ops, SparseCore 0:
  23.3 41.0 reduce-scatter.1
  81.7 33.3 reduce-scatter.1
  132.4 32.9 reduce-scatter.1
  183.1 33.2 reduce-scatter.1
  233.8 33.3 reduce-scatter.1
Sparse Core Ops, SparseCore 1:
  578.6 175.5 all-reduce.4
where the time goes:
time: 778 us; the launch traced here: 764 us
  waiting for transfers between devices  352 us (45%)
  local copies, waits for them, and re-layouts  127 us (16%)
  blocking collectives  95.8 us (12%)
  starting transfers between devices  76.9 us (10%)
  other arithmetic  71.5 us (9%)
  matrix products  23.3 us (3%)
  between operations  15.2 us (2%)
    psum x1, waiting for transfers between devices, body(): grad_sum = lax.psum(grad_total, 'dp')  176 us
    reduce_scatter x5, waiting for transfers between devices, forward_tick(): lax.psum_scatter(lax.dot_general(weight_local, columns, (((0, 1), (0, 1))...  171 us
    all_gather x5, blocking collectives, backward_tick(): shard_piece = lax.all_gather(out_grad, 'tensor', axis=0, tiled=True)  95.8 us
    ppermute x10, starting transfers between devices, passed_along(): lax.ppermute(value, axis, [(source, source + steps) for source in range(f...  76.8 us
    another operation x90, local copies, waits for them, and re-layouts, unfold(): return jnp.stack(tap_list, axis=1).reshape(channels, 9, side_len * side_len)  36.5 us
    while x100, local copies, waits for them, and re-layouts  22 us
    scatter-add x35, local copies, waits for them, and re-layouts, fold_back(): padded = padded.at[:, shift_row:shift_row + side_len, shift_col:shift_col...  19.3 us
  transfers between devices with their start and end apart: 16, of which 11 were waited for; matrix products, arithmetic and copies ran while one was open for 8% of the time, Pallas kernels for 0%

commit v1 on v0

v1 whole, which is shorter than its diff:
```python
import functools

import jax
import jax.numpy as jnp
from jax import lax
from jax.experimental import pallas as pl
from jax.experimental.pallas import tpu as pltpu
from jax.sharding import PartitionSpec as P

GROUP = 20
RES = 16
MOD = 65521
MESH = pl.DeviceIdType.MESH


def below_mod(value):
    value = (value >> 16) * 15 + (value & 65535)
    value = (value >> 16) * 15 + (value & 65535)
    return jnp.where(value >= MOD, value - MOD, value)


def group_sums(values_list, group):
    rows, lanes = values_list[0].shape
    groups = rows // group
    parts = []
    for values in values_list:
        while values.shape[1] > 128:
            half = values.shape[1] // 2
            values = values[:, :half] + values[:, half:]
        for g in range(groups):
            first, last = g * group, (g + 1) * group
            start, end = first // 8 * 8, -(-last // 8) * 8
            total = None
            for row in range(start, end, 8):
                tile = values[row : row + 8]
                if row < first or row + 8 > last:
                    place = lax.broadcasted_iota(jnp.int32, tile.shape, 0) + row
                    tile = jnp.where((place >= first) & (place < last), tile, 0.0)
                total = tile if total is None else total + tile
            parts.append(jnp.sum(total, axis=0, keepdims=True))
    sums = jnp.sum(jnp.concatenate(parts, axis=0), axis=1, keepdims=True)
    place = lax.broadcasted_iota(jnp.int32, (rows, 1), 0)
    spread = []
    for index in range(len(values_list)):
        base = index * groups
        result = jnp.broadcast_to(sums[base : base + 1], (rows, 1))
        for g in range(1, groups):
            result = jnp.where(place >= g * group, sums[base + g : base + g + 1], result)
        spread.append(result)
    return spread


def tap_masks(pixels):
    place = lax.broadcasted_iota(jnp.int32, (1, pixels), 1)
    row, col = place // RES, place % RES
    return {-1: (row >= 1, col >= 1), 0: (None, None), 1: (row < RES - 1, col < RES - 1)}


def moved(values, offset):
    pixels = values.shape[1]
    return values if offset % pixels == 0 else pltpu.roll(values, (-offset) % pixels, axis=1)


def kernel(
    sizes,
    latents_ref,
    target_ref,
    base_ref,
    seed_ref,
    steps_ref,
    table_ref,
    out_ref,
    weight,
    weight_t,
    bias,
    part_send,
    part_recv,
    shift_send,
    shift_recv,
    grad_send,
    grad_recv,
    columns,
    normed,
    scale,
    slope,
    held,
    total,
    sum_send,
    sum_recv,
    own_sum,
    part_sem,
    shift_sem,
    grad_sem,
    sum_sem,
    out_sem,
    send_sem,
):
    replicas, sections, shards, latents_here, all_latents = sizes
    dp = lax.axis_index("dp")
    section = lax.axis_index("section")
    shard = lax.axis_index("tensor")
    channels, pixels = held.shape
    wide = weight.shape[1]
    last = sections - 1
    piece = sum_recv.shape[1]
    owners = weight.shape[0] // piece

    barrier = pltpu.get_barrier_semaphore()

    def greet(section_to, skip_own):
        for j in range(1 if skip_own else 0, shards):
            pl.semaphore_signal(
                barrier,
                inc=1,
                device_id={"section": section_to, "tensor": lax.rem(shard + j, shards)},
                device_id_type=MESH,
            )

    @pl.when(section > 0)
    def _():
        greet(section - 1, False)

    @pl.when(section < last)
    def _():
        greet(section + 1, False)

    @pl.when(section == last)
    def _():
        greet(section, True)

    for j in range(1, replicas):
        pl.semaphore_signal(
            barrier, inc=1, device_id={"dp": lax.rem(dp + j, replicas)}, device_id_type=MESH
        )

    seed = seed_ref[0]
    out_channel = lax.broadcasted_iota(jnp.int32, (8, wide), 1)
    out_part = below_mod(out_channel[0:1] * 32749)
    row_channel = lax.broadcasted_iota(jnp.int32, (channels, 128), 0) + shard * channels
    lane = lax.broadcasted_iota(jnp.int32, (channels, 128), 1)
    for tap in range(9):
        first_index = (row_channel * 9 + tap) * wide
        high = first_index >> 16
        low = high * 15 + (first_index & 65535)
        over = low >= MOD
        low = jnp.where(over, low - MOD, low)
        high = jnp.where(over, high + 1, high)
        row_part = below_mod(low * 32749 + high * 12345 + seed)
        for col in range(0, wide, 128):
            size = min(128, wide - col)
            mixed = row_part[:, :size] + out_part[:, col : col + size]
            mixed = jnp.where(low[:, :size] + lane[:, :size] >= MOD - col, mixed + 12345, mixed)
            mixed = jnp.where(mixed >= MOD, mixed - MOD, mixed)
            mixed = jnp.where(mixed >= MOD, mixed - MOD, mixed)
            noise = mixed.astype(jnp.float32) / 65521.0 - 0.5
            weight[tap * channels : (tap + 1) * channels, col : col + size] = (
                base_ref[tap, :, col : col + size].astype(jnp.float32) + 0.02 * noise
            ).astype(jnp.bfloat16)
    weight_t[...] = weight[...].T

    table_step = lax.broadcasted_iota(jnp.int32, table_ref.shape, 1)
    table = table_ref[...].astype(jnp.float32)
    for latent in range(latents_here):
        bias[latent] = jnp.broadcast_to(
            jnp.sum(
                jnp.where(table_step == steps_ref[latent], table, 0.0), axis=1, keepdims=True
            ),
            (channels, 128),
        )

    @pl.when(section == 0)
    def _():
        pl.semaphore_wait(barrier, replicas - 1 + shards)

    @pl.when((section > 0) & (section < last))
    def _():
        pl.semaphore_wait(barrier, replicas - 1 + 2 * shards)

    @pl.when(section == last)
    def _():
        pl.semaphore_wait(barrier, replicas - 1 + 2 * shards - 1)

    masks = tap_masks(pixels)
    count = float(GROUP * pixels)

    def wait_for(ref, sem):
        pltpu.make_async_copy(ref, ref, sem).wait()

    def send(source, place, sent, arrived, device):
        pltpu.make_async_remote_copy(
            src_ref=source,
            dst_ref=place,
            send_sem=sent,
            recv_sem=arrived,
            device_id=device,
            device_id_type=MESH,
        ).start()

    order = [j for j in (4, 3, 5, 2, 6, 1, 7, 0) if j < shards]
    order += [j for j in range(shards) if j not in order]

    def send_parts(latent):
        @pl.when(section < last)
        def _():
            for j in order:
                peer = lax.rem(shard + j, shards)
                send(
                    part_send.at[latent, peer],
                    part_recv.at[0, latent, shard],
                    send_sem.at[0, latent],
                    part_sem.at[0, latent],
                    {"section": section + 1, "tensor": peer},
                )

        @pl.when(section == last)
        def _():
            for j in order:
                peer = lax.rem(shard + j, shards)
                if j:
                    send(
                        part_send.at[latent, peer],
                        part_recv.at[1, latent, shard],
                        send_sem.at[0, latent],
                        part_sem.at[1, latent],
                        {"tensor": peer},
                    )
                else:
                    pltpu.make_async_copy(
                        part_send.at[latent, shard],
                        part_recv.at[1, latent, shard],
                        part_sem.at[1, latent],
                    ).start()

    def summed(phase, latent, start):
        result = start
        for j in range(shards):
            result = result + part_recv[phase, latent, j].astype(jnp.float32)
        return result.astype(jnp.bfloat16)

    def forward(latent):
        @pl.when(section == 0)
        def _():
            held[...] = latents_ref[latent].astype(jnp.float32)

        @pl.when(section > 0)
        def _():
            wait_for(shift_recv.at[latent], shift_sem.at[latent])
            wait_for(part_recv.at[0, latent], part_sem.at[0, latent])
            held[...] = summed(0, latent, shift_recv[latent]).astype(jnp.float32)

        shifted = held[...] + bias[latent][:, 0:1]
        shift_send[latent] = shifted

        @pl.when(section < last)
        def _():
            send(
                shift_send.at[latent],
                shift_recv.at[latent],
                send_sem.at[2, latent],
                shift_sem.at[latent],
                {"section": section + 1},
            )

        (sums,) = group_sums([shifted], GROUP)
        center = shifted - sums / count
        (squares,) = group_sums([center * center], GROUP)
        factor = lax.rsqrt(squares / count + 1e-05)
        value = center * factor
        sigmoid = 1.0 / (1.0 + jnp.exp(-value))
        activation = (value * sigmoid).astype(jnp.bfloat16).astype(jnp.float32)
        for dj in (-1, 0, 1):
            across = moved(activation, dj)
            if dj:
                across = jnp.where(masks[dj][1], across, 0.0)
            for di in (-1, 0, 1):
                tap = (di + 1) * 3 + dj + 1
                both = moved(across, di * RES)
                if di:
                    both = jnp.where(masks[di][0], both, 0.0)
                columns[latent, tap * channels : (tap + 1) * channels] = both.astype(jnp.bfloat16)
        part_send[latent] = (
            jnp.dot(weight_t[...], columns[latent], preferred_element_type=jnp.float32)
            .astype(jnp.bfloat16)
            .reshape(shards, channels, pixels)
        )
        send_parts(latent)
        normed[latent] = value
        scale[latent] = jnp.broadcast_to(factor, (channels, 128))
        slope[latent] = sigmoid * (1.0 + value * (1.0 - sigmoid))

    for latent in range(latents_here):
        forward(latent)

    grad_back = grad_send.at[1]
    grad_first = grad_send.at[0]

    for latent in range(latents_here):

        @pl.when(section == last)
        def _(latent=latent):
            wait_for(part_recv.at[1, latent], part_sem.at[1, latent])
            output = summed(1, latent, shift_send[latent]).astype(jnp.float32)
            grad_first[latent] = (
                (output - target_ref[latent].astype(jnp.float32)) / float(all_latents)
            ).astype(jnp.bfloat16)
            for j in order:
                peer = lax.rem(shard + j, shards)
                if j:
                    send(
                        grad_first.at[latent],
                        grad_recv.at[latent, shard],
                        send_sem.at[3, latent],
                        grad_sem.at[latent],
                        {"tensor": peer},
                    )
                else:
                    pltpu.make_async_copy(
                        grad_first.at[latent], grad_recv.at[latent, shard], grad_sem.at[latent]
                    ).start()

        wait_for(grad_recv.at[latent], grad_sem.at[latent])
        out_grad = grad_recv[latent].reshape(wide, pixels)

        @pl.when(section > 0)
        def _(latent=latent, out_grad=out_grad):
            spread = jnp.dot(weight[...], out_grad, preferred_element_type=jnp.float32)
            col_grad = None
            for dj in (-1, 0, 1):
                down = None
                for di in (-1, 0, 1):
                    tap = (di + 1) * 3 + dj + 1
                    term = spread[tap * channels : (tap + 1) * channels]
                    if di:
                        term = moved(jnp.where(masks[di][0], term, 0.0), -di * RES)
                    down = term if down is None else down + term
                if dj:
                    down = moved(jnp.where(masks[dj][1], down, 0.0), -dj)
                col_grad = down if col_grad is None else col_grad + down
            value = normed[latent]
            inner = col_grad * slope[latent]
            mean_inner, mean_both = group_sums([inner, inner * value], GROUP)
            in_grad = scale[latent][:, 0:1] * (
                inner - mean_inner / count - value * (mean_both / count)
            )
            grad_back[latent] = (
                grad_recv[latent, shard].astype(jnp.float32) + in_grad
            ).astype(jnp.bfloat16)
            for j in order:
                send(
                    grad_back.at[latent],
                    grad_recv.at[latent, shard],
                    send_sem.at[1, latent],
                    grad_sem.at[latent],
                    {"section": section - 1, "tensor": lax.rem(shard + j, shards)},
                )

        part = lax.dot_general(
            columns[latent], out_grad, (((1,), (1,)), ((), ())), preferred_element_type=jnp.float32
        )
        if latent == 0 and latents_here > 1:
            total[...] = part
        elif latent < latents_here - 1:
            total[...] += part
        else:
            if latent:
                part = total[...] + part
            sum_send[...] = part.astype(jnp.bfloat16)

    for j in range(1, replicas + 1):
        owner = lax.rem(dp + j, replicas)
        rows = pl.ds(pl.multiple_of(owner * piece, 16), piece)

        @pl.when(owner < owners)
        def _(j=j, owner=owner, rows=rows):
            if j < replicas:
                send(
                    sum_send.at[rows], sum_recv.at[dp], send_sem.at[4, 0], sum_sem, {"dp": owner}
                )
            else:
                pltpu.make_async_copy(sum_send.at[rows], sum_recv.at[dp], sum_sem).start()

    @pl.when(dp < owners)
    def _():
        wait_for(sum_recv, sum_sem)
        result = sum_recv[0].astype(jnp.float32)
        for j in range(1, replicas):
            result = result + sum_recv[j].astype(jnp.float32)
        own_sum[...] = result.astype(jnp.bfloat16)
        rows = pl.ds(pl.multiple_of(dp * piece, 16), piece)
        for j in range(1, replicas + 1):
            if j < replicas:
                send(
                    own_sum,
                    out_ref.at[rows],
                    send_sem.at[4, 1],
                    out_sem,
                    {"dp": lax.rem(dp + j, replicas)},
                )
            else:
                pltpu.make_async_copy(own_sum, out_ref.at[rows], out_sem).start()

    for latent in range(latents_here):

        @pl.when(section < last)
        def _(latent=latent):
            wait_for(part_send.at[latent], send_sem.at[0, latent])
            wait_for(shift_send.at[latent], send_sem.at[2, latent])

        @pl.when(section == last)
        def _(latent=latent):
            others = part_send.at[latent, pl.ds(0, shards - 1)]
            wait_for(others, send_sem.at[0, latent])
            wait_for(others, send_sem.at[3, latent])

        @pl.when(section > 0)
        def _(latent=latent):
            wait_for(part_send.at[latent], send_sem.at[1, latent])

    @pl.when(dp < owners)
    def _():
        wait_for(sum_send.at[pl.ds(0, (owners - 1) * piece)], send_sem.at[4, 0])
        wait_for(sum_recv.at[pl.ds(0, replicas - 1)], send_sem.at[4, 1])

    @pl.when(dp >= owners)
    def _():
        wait_for(sum_send, send_sem.at[4, 0])

    wait_for(out_ref, out_sem)


def body(latents, target, base_weight, seeds, timesteps, time_table):
    replicas, sections, shards = (lax.axis_size(name) for name in ("dp", "section", "tensor"))
    channels, latents_here, pixels = latents.shape
    wide = base_weight.shape[3]
    rows = 9 * channels
    owners = max(n for n in range(1, replicas + 1) if (rows // 16) % n == 0)
    sizes = (replicas, sections, shards, latents_here, latents_here * replicas)
    vmem = pl.BlockSpec(memory_space=pltpu.VMEM)
    smem = pl.BlockSpec(memory_space=pltpu.SMEM)
    bf16, f32 = jnp.bfloat16, jnp.float32
    here = latents_here
    scratch = [
        pltpu.VMEM((rows, wide), bf16),
        pltpu.VMEM((wide, rows), bf16),
        pltpu.VMEM((here, channels, 128), f32),
        pltpu.VMEM((here, shards, channels, pixels), bf16),
        pltpu.VMEM((2, here, shards, channels, pixels), bf16),
        pltpu.VMEM((here, channels, pixels), f32),
        pltpu.VMEM((here, channels, pixels), f32),
        pltpu.VMEM((2, here, channels, pixels), bf16),
        pltpu.VMEM((here, shards, channels, pixels), bf16),
        pltpu.VMEM((here, rows, pixels), bf16),
        pltpu.VMEM((here, channels, pixels), f32),
        pltpu.VMEM((here, channels, 128), f32),
        pltpu.VMEM((here, channels, pixels), f32),
        pltpu.VMEM((channels, pixels), f32),
        pltpu.VMEM((rows, wide), f32),
        pltpu.VMEM((rows, wide), bf16),
        pltpu.VMEM((replicas, rows // owners, wide), bf16),
        pltpu.VMEM((rows // owners, wide), bf16),
        pltpu.SemaphoreType.DMA((2, here)),
        pltpu.SemaphoreType.DMA((here,)),
        pltpu.SemaphoreType.DMA((here,)),
        pltpu.SemaphoreType.DMA,
        pltpu.SemaphoreType.DMA,
        pltpu.SemaphoreType.DMA((5, 2)),
    ]
    result = pl.pallas_call(
        functools.partial(kernel, sizes),
        out_shape=jax.ShapeDtypeStruct((rows, wide), bf16),
        in_specs=[vmem, vmem, vmem, smem, smem, vmem],
        out_specs=vmem,
        scratch_shapes=scratch,
        compiler_params=pltpu.CompilerParams(
            collective_id=0, has_side_effects=True, vmem_limit_bytes=48 * 1024 * 1024
        ),
        cost_estimate=pl.CostEstimate(
            flops=6 * here * rows * wide * pixels, bytes_accessed=4 * rows * wide, transcendentals=0
        ),
    )(
        latents.transpose(1, 0, 2),
        target.transpose(1, 0, 2),
        base_weight[0].transpose(1, 0, 2),
        seeds,
        timesteps,
        time_table[0].T,
    )
    return result.astype(f32).reshape(9, channels, wide).transpose(1, 0, 2)[None]


def solution(mesh):
    in_specs = (
        P("tensor", "dp", None),
        P("tensor", "dp", None),
        P("section", "tensor", None, None),
        P("section"),
        P("dp"),
        P("section", None, "tensor"),
    )
    out_specs = P("section", "tensor", None, None)
    return jax.shard_map(body, mesh=mesh, in_specs=in_specs, out_specs=out_specs, check_vma=False)
```

time: 778 us -> 133 us (0.17); the launches traced: 764 us -> 133 us
  waiting for transfers between devices: 352 us -> 0 us
  Pallas kernels: 0 us -> 127 us
  local copies, waits for them, and re-layouts: 127 us -> 3.69 us
  blocking collectives: 95.8 us -> 0 us
  starting transfers between devices: 76.9 us -> 0 us
  other arithmetic: 71.5 us -> 1.35 us
  matrix products: 23.3 us -> 0 us
  between operations: 15.2 us -> 0.67 us
    psum x1 -> x0, waiting for transfers between devices: 176 us -> none  [body(): grad_sum = lax.psum(grad_total, 'dp')]
    reduce_scatter x5 -> x0, waiting for transfers between devices: 171 us -> none  [forward_tick(): lax.psum_scatter(lax.dot_general(weight_local, columns, (((0, 1), (0, 1))...]
    pallas_call x0 -> x1, Pallas kernels: none -> 127 us  [body(): pl.pallas_call(functools.partial(kernel, sizes), out_shape=jax.ShapeDtype...]
    all_gather x5 -> x0, blocking collectives: 95.8 us -> none  [backward_tick(): shard_piece = lax.all_gather(out_grad, 'tensor', axis=0, tiled=True)]
    ppermute x10 -> x0, starting transfers between devices: 76.8 us -> none  [passed_along(): lax.ppermute(value, axis, [(source, source + steps) for source in range(f...]
    another operation x107 -> x0, local copies, waits for them, and re-layouts: 43.2 us -> none  [the longest x90 36.5 us: unfold(): return jnp.stack(tap_list, axis=1).reshape(channels, 9, side_len * side_len)]
    while x102 -> x0, local copies, waits for them, and re-layouts: 23.8 us -> none
    dot_general x25 -> x0, matrix products: 23.3 us -> none  [the longest x10 11 us: lookup(): jnp.dot(onehot[None, :], steps_table, preferred_element_type=jnp.float32)[0]]
  transfers between devices with their start and end apart: 16 -> 0, of which waited for: 11 -> 0; matrix products, arithmetic and copies ran while one was open for 8% -> 0% of each run, Pallas kernels for 0% -> 0%
where the time goes in v1:
time: 133 us
  Pallas kernels  127 us (95%)
  local copies, waits for them, and re-layouts  3.69 us (3%)
  other arithmetic  1.35 us (1%)
    pallas_call x1, Pallas kernels, body(): pl.pallas_call(functools.partial(kernel, sizes), out_shape=jax.ShapeDtype...  127 us
    unnamed x6, local copies, waits for them, and re-layouts  2.75 us

profile of v1, /device:TPU:1, one launch (start us, length us, event | category | flops | bytes accessed | tf_op | source)
XLA Modules:
  0.0 133.2 jit_solution(7131023027456549196)
XLA Ops:
  0.7 0.9 copy_bitcast_fusion
  1.6 0.0 copy-start
  1.6 1.2 copy-done
  2.8 0.0 copy-start.1
  2.8 0.9 copy-done.1
  3.7 0.0 copy-start.2
  3.7 0.7 copy-done.2
  4.4 127.5 %shard_map.64 = bf16[720,640]{1,0:T(8,128)(2,1)S(1)} custom-call(bf16[2,80,256]{2,1,0:T(8,128)(2,1)S(1)} %get-tuple-element.6.latents_ref, bf16[2,80,256]{2,1,0:T(8,128)(2,1)S(1)} %get-tuple-element.5.target_ref, bf16[9,80,640]{2,1,0:T(8,128)(2,1)S(1)} %bitcast.17, s32[1]{0:T(128)S(6)} %copy.11.seed_ref, s32[2]{0:T(128)S(1)} %copy-done.2, ...), custom_call_target="tpu_custom_call" | custom-call | flops 1415577600 | bytes 1843200 | tf_op jit(solution)/shard_map/pallas_call | solution.py:468
  131.8 1.4 %convert_bitcast_fusion = f32[1,80,9,640]{3,1,2,0:T(8,128)} fusion(bf16[9,80,640]{2,1,0:T(8,128)(2,1)S(1)} %bitcast.16), kind=kLoop, calls=%fused_computation | loop fusion | flops 460800 | bytes 2764800 | tf_op jit(solution)/shard_map/broadcast_in_dim | solution.py:488
Async XLA Ops:
  1.6 1.2 copy-start
  2.8 0.9 copy-start.1
  3.7 0.7 copy-start.2

commit v2 on v1

--- a/solution.py
+++ b/solution.py
@@ -10,6 +10,8 @@
 GROUP = 20
 RES = 16
 MOD = 65521
+CHUNK = 16
+SIDE = 4
 MESH = pl.DeviceIdType.MESH
 
 
@@ -63,13 +65,18 @@
 
 def kernel(
     sizes,
+    latents_hbm,
+    target_hbm,
+    base_hbm,
+    seed_ref,
+    steps_ref,
+    table_hbm,
+    out_ref,
     latents_ref,
     target_ref,
     base_ref,
-    seed_ref,
-    steps_ref,
     table_ref,
-    out_ref,
+    load_sem,
     weight,
     weight_t,
     bias,
@@ -88,6 +95,8 @@
     sum_send,
     sum_recv,
     own_sum,
+    across_recv,
+    across_sum,
     part_sem,
     shift_sem,
     grad_sem,
@@ -103,7 +112,21 @@
     wide = weight.shape[1]
     last = sections - 1
     piece = sum_recv.shape[1]
-    owners = weight.shape[0] // piece
+    chunks = [(start, min(CHUNK, piece - start)) for start in range(0, piece, CHUNK)]
+
+    loads = [
+        pltpu.make_async_copy(source, place, load_sem.at[n])
+        for n, (source, place) in enumerate(
+            [
+                (base_hbm, base_ref),
+                (table_hbm, table_ref),
+                (latents_hbm, latents_ref),
+                (target_hbm, target_ref),
+            ]
+        )
+    ]
+    for load in loads:
+        load.start()
 
     barrier = pltpu.get_barrier_semaphore()
 
@@ -132,6 +155,9 @@
         pl.semaphore_signal(
             barrier, inc=1, device_id={"dp": lax.rem(dp + j, replicas)}, device_id_type=MESH
         )
+
+    for load in loads:
+        load.wait()
 
     seed = seed_ref[0]
     out_channel = lax.broadcasted_iota(jnp.int32, (8, wide), 1)
@@ -318,6 +344,7 @@
                         grad_first.at[latent], grad_recv.at[latent, shard], grad_sem.at[latent]
                     ).start()
 
+    for latent in range(latents_here):
         wait_for(grad_recv.at[latent], grad_sem.at[latent])
         out_grad = grad_recv[latent].reshape(wide, pixels)
 
@@ -364,40 +391,89 @@
         else:
             if latent:
                 part = total[...] + part
-            sum_send[...] = part.astype(jnp.bfloat16)
-
-    for j in range(1, replicas + 1):
-        owner = lax.rem(dp + j, replicas)
-        rows = pl.ds(pl.multiple_of(owner * piece, 16), piece)
-
-        @pl.when(owner < owners)
-        def _(j=j, owner=owner, rows=rows):
-            if j < replicas:
-                send(
-                    sum_send.at[rows], sum_recv.at[dp], send_sem.at[4, 0], sum_sem, {"dp": owner}
-                )
+            rows = part.shape[0]
+            sum_send[:rows] = part.astype(jnp.bfloat16)
+            if rows < sum_send.shape[0]:
+                sum_send[rows:] = jnp.zeros((sum_send.shape[0] - rows, wide), jnp.bfloat16)
+
+    def added(ref, rows):
+        result = ref[0, rows].astype(jnp.float32)
+        for j in range(1, ref.shape[0]):
+            result = result + ref[j, rows].astype(jnp.float32)
+        return result.astype(jnp.bfloat16)
+
+    def part_rows(start, size):
+        return pl.ds(pl.multiple_of(start, 16), size)
+
+    @pl.when(section == 0)
+    def _():
+        for c, (start, size) in enumerate(chunks):
+            for j in range(1, replicas + 1):
+                owner = lax.rem(dp + j, replicas)
+                source = sum_send.at[part_rows(owner * piece + start, size)]
+                place = sum_recv.at[dp, pl.ds(start, size)]
+                if j < replicas:
+                    send(source, place, send_sem.at[4, 0], sum_sem.at[c], {"dp": owner})
+                else:
+                    pltpu.make_async_copy(source, place, sum_sem.at[c]).start()
+        for c, (start, size) in enumerate(chunks):
+            rows = pl.ds(start, size)
+            wait_for(sum_recv.at[:, rows], sum_sem.at[c])
+            own_sum[rows] = added(sum_recv, rows)
+            place = out_ref.at[part_rows(dp * piece + start, size)]
+            for j in range(1, replicas + 1):
+                if j < replicas:
+                    other = {"dp": lax.rem(dp + j, replicas)}
+                    send(own_sum.at[rows], place, send_sem.at[4, 1], out_sem.at[0], other)
+                else:
+                    pltpu.make_async_copy(own_sum.at[rows], place, out_sem.at[0]).start()
+        wait_for(out_ref, out_sem.at[0])
+        wait_for(sum_recv.at[pl.ds(0, replicas - 1)], send_sem.at[4, 0])
+        wait_for(sum_recv.at[pl.ds(0, replicas - 1)], send_sem.at[4, 1])
+
+    @pl.when(section > 0)
+    def _():
+        side = across_recv.shape[0]
+        other_side = replicas // side
+        strip = piece * other_side
+        x, y = dp // other_side, lax.rem(dp, other_side)
+        for j in range(1, side + 1):
+            to = lax.rem(x + j, side)
+            source, place = sum_send.at[part_rows(to * strip, strip)], across_recv.at[x]
+            if j < side:
+                device = {"dp": to * other_side + y}
+                send(source, place, send_sem.at[4, 0], sum_sem.at[0], device)
             else:
-                pltpu.make_async_copy(sum_send.at[rows], sum_recv.at[dp], sum_sem).start()
-
-    @pl.when(dp < owners)
-    def _():
-        wait_for(sum_recv, sum_sem)
-        result = sum_recv[0].astype(jnp.float32)
-        for j in range(1, replicas):
-            result = result + sum_recv[j].astype(jnp.float32)
-        own_sum[...] = result.astype(jnp.bfloat16)
-        rows = pl.ds(pl.multiple_of(dp * piece, 16), piece)
-        for j in range(1, replicas + 1):
-            if j < replicas:
-                send(
-                    own_sum,
-                    out_ref.at[rows],
-                    send_sem.at[4, 1],
-                    out_sem,
-                    {"dp": lax.rem(dp + j, replicas)},
-                )
+                pltpu.make_async_copy(source, place, sum_sem.at[0]).start()
+        wait_for(across_recv, sum_sem.at[0])
+        across_sum[...] = added(across_recv, pl.ds(0, strip))
+        for j in range(1, other_side + 1):
+            to = lax.rem(y + j, other_side)
+            source, place = across_sum.at[part_rows(to * piece, piece)], sum_recv.at[y]
+            if j < other_side:
+                device = {"dp": x * other_side + to}
+                send(source, place, send_sem.at[4, 1], sum_sem.at[1], device)
             else:
-                pltpu.make_async_copy(own_sum, out_ref.at[rows], out_sem).start()
+                pltpu.make_async_copy(source, place, sum_sem.at[1]).start()
+        wait_for(sum_recv.at[pl.ds(0, other_side)], sum_sem.at[1])
+        own_sum[...] = added(sum_recv.at[pl.ds(0, other_side)], pl.ds(0, piece))
+        place = out_ref.at[part_rows(dp * piece, piece)]
+        for j in range(1, other_side + 1):
+            if j < other_side:
+                device = {"dp": x * other_side + lax.rem(y + j, other_side)}
+                send(own_sum, place, send_sem.at[5, 0], out_sem.at[0], device)
+            else:
+                pltpu.make_async_copy(own_sum, place, out_sem.at[0]).start()
+        mine = out_ref.at[part_rows(x * strip, strip)]
+        wait_for(mine, out_sem.at[0])
+        for j in range(1, side):
+            device = {"dp": lax.rem(x + j, side) * other_side + y}
+            send(mine, mine, send_sem.at[5, 1], out_sem.at[1], device)
+        wait_for(across_recv.at[pl.ds(0, side - 1)], out_sem.at[1])
+        wait_for(across_recv.at[pl.ds(0, side - 1)], send_sem.at[4, 0])
+        wait_for(across_recv.at[pl.ds(0, side - 1)], send_sem.at[5, 1])
+        wait_for(sum_recv.at[pl.ds(0, other_side - 1)], send_sem.at[4, 1])
+        wait_for(sum_recv.at[pl.ds(0, other_side - 1)], send_sem.at[5, 0])
 
     for latent in range(latents_here):
 
@@ -416,30 +492,27 @@
         def _(latent=latent):
             wait_for(part_send.at[latent], send_sem.at[1, latent])
 
-    @pl.when(dp < owners)
-    def _():
-        wait_for(sum_send.at[pl.ds(0, (owners - 1) * piece)], send_sem.at[4, 0])
-        wait_for(sum_recv.at[pl.ds(0, replicas - 1)], send_sem.at[4, 1])
-
-    @pl.when(dp >= owners)
-    def _():
-        wait_for(sum_send, send_sem.at[4, 0])
-
-    wait_for(out_ref, out_sem)
-
 
 def body(latents, target, base_weight, seeds, timesteps, time_table):
     replicas, sections, shards = (lax.axis_size(name) for name in ("dp", "section", "tensor"))
     channels, latents_here, pixels = latents.shape
     wide = base_weight.shape[3]
     rows = 9 * channels
-    owners = max(n for n in range(1, replicas + 1) if (rows // 16) % n == 0)
+    piece = -(-rows // (16 * replicas)) * 16
+    side = min(SIDE, replicas)
+    strip = piece * (replicas // side)
     sizes = (replicas, sections, shards, latents_here, latents_here * replicas)
     vmem = pl.BlockSpec(memory_space=pltpu.VMEM)
     smem = pl.BlockSpec(memory_space=pltpu.SMEM)
+    hbm = pl.BlockSpec(memory_space=pl.ANY)
     bf16, f32 = jnp.bfloat16, jnp.float32
     here = latents_here
     scratch = [
+        pltpu.VMEM((here, channels, pixels), bf16),
+        pltpu.VMEM((here, channels, pixels), bf16),
+        pltpu.VMEM((9, channels, wide), bf16),
+        pltpu.VMEM(time_table.shape[:0:-1], bf16),
+        pltpu.SemaphoreType.DMA((4,)),
         pltpu.VMEM((rows, wide), bf16),
         pltpu.VMEM((wide, rows), bf16),
         pltpu.VMEM((here, channels, 128), f32),
@@ -455,20 +528,22 @@
         pltpu.VMEM((here, channels, pixels), f32),
         pltpu.VMEM((channels, pixels), f32),
         pltpu.VMEM((rows, wide), f32),
-        pltpu.VMEM((rows, wide), bf16),
-        pltpu.VMEM((replicas, rows // owners, wide), bf16),
-        pltpu.VMEM((rows // owners, wide), bf16),
+        pltpu.VMEM((replicas * piece, wide), bf16),
+        pltpu.VMEM((replicas, piece, wide), bf16),
+        pltpu.VMEM((piece, wide), bf16),
+        pltpu.VMEM((side, strip, wide), bf16),
+        pltpu.VMEM((strip, wide), bf16),
         pltpu.SemaphoreType.DMA((2, here)),
         pltpu.SemaphoreType.DMA((here,)),
         pltpu.SemaphoreType.DMA((here,)),
-        pltpu.SemaphoreType.DMA,
-        pltpu.SemaphoreType.DMA,
-        pltpu.SemaphoreType.DMA((5, 2)),
+        pltpu.SemaphoreType.DMA((max(2, -(-piece // CHUNK)),)),
+        pltpu.SemaphoreType.DMA((2,)),
+        pltpu.SemaphoreType.DMA((6, 2)),
     ]
     result = pl.pallas_call(
         functools.partial(kernel, sizes),
-        out_shape=jax.ShapeDtypeStruct((rows, wide), bf16),
-        in_specs=[vmem, vmem, vmem, smem, smem, vmem],
+        out_shape=jax.ShapeDtypeStruct((replicas * piece, wide), bf16),
+        in_specs=[hbm, hbm, hbm, smem, smem, hbm],
         out_specs=vmem,
         scratch_shapes=scratch,
         compiler_params=pltpu.CompilerParams(
@@ -485,7 +560,7 @@
         timesteps,
         time_table[0].T,
     )
-    return result.astype(f32).reshape(9, channels, wide).transpose(1, 0, 2)[None]
+    return result[:rows].astype(f32).reshape(9, channels, wide).transpose(1, 0, 2)[None]
 
 
 def solution(mesh):

time: 133 us -> 118 us (0.89)
  Pallas kernels: 127 us -> 112 us
    pallas_call x1, Pallas kernels: 127 us -> 112 us  [body(): pl.pallas_call(functools.partial(kernel, sizes), out_shape=jax.ShapeDtype...]
where the time goes in v2:
time: 118 us
  Pallas kernels  112 us (95%)
  local copies, waits for them, and re-layouts  3.77 us (3%)
  other arithmetic  1.35 us (1%)
    pallas_call x1, Pallas kernels, body(): pl.pallas_call(functools.partial(kernel, sizes), out_shape=jax.ShapeDtype...  112 us
    unnamed x6, local copies, waits for them, and re-layouts  2.75 us

profile of v2, /device:TPU:1, one launch (start us, length us, event | category | flops | bytes accessed | tf_op | source)
XLA Modules:
  0.0 117.9 jit_solution(8409211542190344183)
XLA Ops:
  0.7 0.9 copy_bitcast_fusion
  1.6 0.0 copy-start
  1.6 1.2 copy-done
  2.8 0.0 copy-start.1
  2.8 0.9 copy-done.1
  3.7 0.0 copy-start.2
  3.7 0.7 copy-done.2
  4.4 112.1 %shard_map.64 = bf16[768,640]{1,0:T(8,128)(2,1)S(1)} custom-call(bf16[2,80,256]{2,1,0:T(8,128)(2,1)S(1)} %get-tuple-element.6.latents_hbm, bf16[2,80,256]{2,1,0:T(8,128)(2,1)S(1)} %get-tuple-element.5.target_hbm, bf16[9,80,640]{2,1,0:T(8,128)(2,1)S(1)} %bitcast.16, s32[1]{0:T(128)S(6)} %copy.11.seed_ref, s32[2]{0:T(128)S(1)} %copy-done.2, ...), custom_call_target="tpu_custom_call" | custom-call | flops 1415577600 | bytes 1843200 | tf_op jit(solution)/shard_map/pallas_call | solution.py:543
  116.4 0.1 slice.3
  116.5 1.4 %convert_bitcast_fusion = f32[1,80,9,640]{3,1,2,0:T(8,128)} fusion(bf16[9,80,640]{2,1,0:T(8,128)(2,1)S(1)} %bitcast.18), kind=kLoop, calls=%fused_computation | loop fusion | flops 460800 | bytes 2764800 | tf_op jit(solution)/shard_map/broadcast_in_dim | solution.py:563
Async XLA Ops:
  1.6 1.2 %copy-start = (bf16[1,80,9,640]{3,1,2,0:T(8,128)(2,1)S(1)}, bf16[1,80,9,640]{3,1,2,0:T(8,128)(2,1)}, u32[]{:S(2)}) copy-start(bf16[1,80,9,640]{3,1,2,0:T(8,128)(2,1)} %param.8) | copy-start | bytes 2764804
  2.8 0.9 copy-start.1
  3.7 0.7 copy-start.2

commit v3 on v2

v3 whole, which is shorter than its diff:
```python
import functools

import jax
import jax.numpy as jnp
from jax import lax
from jax.experimental import pallas as pl
from jax.experimental.pallas import tpu as pltpu
from jax.sharding import PartitionSpec as P

GROUP = 20
RES = 16
MOD = 65521
PIECES = (32, 16)
SIDE = 4
MESH = pl.DeviceIdType.MESH


def below_mod(value):
    value = (value >> 16) * 15 + (value & 65535)
    value = (value >> 16) * 15 + (value & 65535)
    return jnp.where(value >= MOD, value - MOD, value)


def group_sums(values_list, group):
    rows, lanes = values_list[0].shape
    groups = rows // group
    parts = []
    for values in values_list:
        while values.shape[1] > 128:
            half = values.shape[1] // 2
            values = values[:, :half] + values[:, half:]
        for g in range(groups):
            first, last = g * group, (g + 1) * group
            start, end = first // 8 * 8, -(-last // 8) * 8
            total = None
            for row in range(start, end, 8):
                tile = values[row : row + 8]
                if row < first or row + 8 > last:
                    place = lax.broadcasted_iota(jnp.int32, tile.shape, 0) + row
                    tile = jnp.where((place >= first) & (place < last), tile, 0.0)
                total = tile if total is None else total + tile
            parts.append(jnp.sum(total, axis=0, keepdims=True))
    sums = jnp.sum(jnp.concatenate(parts, axis=0), axis=1, keepdims=True)
    place = lax.broadcasted_iota(jnp.int32, (rows, 1), 0)
    spread = []
    for index in range(len(values_list)):
        base = index * groups
        result = jnp.broadcast_to(sums[base : base + 1], (rows, 1))
        for g in range(1, groups):
            result = jnp.where(place >= g * group, sums[base + g : base + g + 1], result)
        spread.append(result)
    return spread


def tap_masks(pixels):
    place = lax.broadcasted_iota(jnp.int32, (1, pixels), 1)
    row, col = place // RES, place % RES
    return {-1: (row >= 1, col >= 1), 0: (None, None), 1: (row < RES - 1, col < RES - 1)}


def moved(values, offset):
    pixels = values.shape[1]
    return values if offset % pixels == 0 else pltpu.roll(values, (-offset) % pixels, axis=1)


def kernel(
    sizes,
    latents_hbm,
    target_hbm,
    base_hbm,
    seed_hbm,
    steps_hbm,
    table_hbm,
    out_ref,
    latents_ref,
    target_ref,
    base_ref,
    table_ref,
    seed_ref,
    steps_ref,
    load_sem,
    weight,
    weight_t,
    bias,
    part_send,
    part_recv,
    shift_send,
    shift_recv,
    grad_send,
    grad_recv,
    columns,
    normed,
    scale,
    slope,
    held,
    total,
    sum_send,
    sum_recv,
    own_sum,
    across_recv,
    across_sum,
    sum_done,
    down_sem,
    up_sem,
    part_sem,
    shift_sem,
    grad_sem,
    sum_sem,
    out_sem,
    send_sem,
):
    replicas, sections, shards, latents_here, all_latents = sizes
    dp = lax.axis_index("dp")
    section = lax.axis_index("section")
    shard = lax.axis_index("tensor")
    channels, pixels = held.shape
    wide = weight.shape[1]
    last = sections - 1
    side = across_recv.shape[0]
    other_side = replicas // side
    x, y = dp // other_side, lax.rem(dp, other_side)
    chunks, start = [], 0
    for piece in PIECES:
        chunks.append((start, piece))
        start += piece * replicas

    loads = [
        pltpu.make_async_copy(source, place, load_sem.at[n])
        for n, (source, place) in enumerate(
            [
                (steps_hbm, steps_ref),
                (seed_hbm, seed_ref),
                (table_hbm, table_ref),
                (latents_hbm, latents_ref),
                (base_hbm, base_ref),
                (target_hbm, target_ref),
            ]
        )
    ]
    for load in loads:
        load.start()

    barrier = pltpu.get_barrier_semaphore()

    def greet(section_to, skip_own):
        for j in range(1 if skip_own else 0, shards):
            peer = lax.rem(shard + j, shards)
            pl.semaphore_signal(
                barrier,
                inc=1,
                device_id={"section": section_to, "tensor": peer},
                device_id_type=MESH,
            )

    @pl.when(section > 0)
    def _():
        greet(section - 1, False)

    @pl.when(section < last)
    def _():
        greet(section + 1, False)

    @pl.when(section == last)
    def _():
        greet(section, True)

    for j in range(1, replicas):
        pl.semaphore_signal(
            barrier, inc=1, device_id={"dp": lax.rem(dp + j, replicas)}, device_id_type=MESH
        )

    masks = tap_masks(pixels)
    count = float(GROUP * pixels)

    def wait_for(ref, sem):
        pltpu.make_async_copy(ref, ref, sem).wait()

    def send(source, place, sent, arrived, device):
        pltpu.make_async_remote_copy(
            src_ref=source,
            dst_ref=place,
            send_sem=sent,
            recv_sem=arrived,
            device_id=device,
            device_id_type=MESH,
        ).start()

    order = [j for j in (4, 3, 5, 2, 6, 1, 7, 0) if j < shards]
    order += [j for j in range(shards) if j not in order]

    def send_parts(latent):
        @pl.when(section < last)
        def _():
            for j in order:
                peer = lax.rem(shard + j, shards)
                send(
                    part_send.at[latent, peer],
                    part_recv.at[0, latent, shard],
                    send_sem.at[0, latent],
                    part_sem.at[0, latent],
                    {"section": section + 1, "tensor": peer},
                )

        @pl.when(section == last)
        def _():
            for j in order:
                peer = lax.rem(shard + j, shards)
                if j:
                    send(
                        part_send.at[latent, peer],
                        part_recv.at[1, latent, shard],
                        send_sem.at[0, latent],
                        part_sem.at[1, latent],
                        {"tensor": peer},
                    )
                else:
                    pltpu.make_async_copy(
                        part_send.at[latent, shard],
                        part_recv.at[1, latent, shard],
                        part_sem.at[1, latent],
                    ).start()

    def summed(phase, latent, start):
        result = start
        for j in range(shards):
            result = result + part_recv[phase, latent, j].astype(jnp.float32)
        return result.astype(jnp.bfloat16)

    def take(latent):
        @pl.when(section == 0)
        def _():
            held[...] = latents_ref[latent].astype(jnp.float32)

        @pl.when(section > 0)
        def _():
            wait_for(shift_recv.at[latent], shift_sem.at[latent])
            wait_for(part_recv.at[0, latent], part_sem.at[0, latent])
            held[...] = summed(0, latent, shift_recv[latent]).astype(jnp.float32)

        shift_send[latent] = held[...] + bias[latent][:, 0:1]

    def send_shift(latent):
        @pl.when(section < last)
        def _():
            send(
                shift_send.at[latent],
                shift_recv.at[latent],
                send_sem.at[2, latent],
                shift_sem.at[latent],
                {"section": section + 1},
            )

    def activate(latent):
        shifted = shift_send[latent]
        (sums,) = group_sums([shifted], GROUP)
        center = shifted - sums / count
        (squares,) = group_sums([center * center], GROUP)
        factor = lax.rsqrt(squares / count + 1e-05)
        value = center * factor
        sigmoid = 1.0 / (1.0 + jnp.exp(-value))
        activation = (value * sigmoid).astype(jnp.bfloat16).astype(jnp.float32)
        for dj in (-1, 0, 1):
            across = moved(activation, dj)
            if dj:
                across = jnp.where(masks[dj][1], across, 0.0)
            for di in (-1, 0, 1):
                tap = (di + 1) * 3 + dj + 1
                both = moved(across, di * RES)
                if di:
                    both = jnp.where(masks[di][0], both, 0.0)
                columns[latent, tap * channels : (tap + 1) * channels] = both.astype(jnp.bfloat16)
        normed[latent] = value
        slope[latent] = sigmoid
        scale[latent] = jnp.broadcast_to(factor, (channels, 128))

    def emit(latent):
        part_send[latent] = (
            jnp.dot(weight_t[...], columns[latent], preferred_element_type=jnp.float32)
            .astype(jnp.bfloat16)
            .reshape(shards, channels, pixels)
        )
        send_parts(latent)
        sigmoid = slope[latent]
        slope[latent] = sigmoid * (1.0 + normed[latent] * (1.0 - sigmoid))

    loads[0].wait()
    loads[2].wait()
    loads[3].wait()
    table_step = lax.broadcasted_iota(jnp.int32, table_ref.shape, 1)
    table = table_ref[...].astype(jnp.float32)
    for latent in range(latents_here):
        picked = jnp.where(table_step == steps_ref[latent], table, 0.0)
        own_bias = jnp.broadcast_to(jnp.sum(picked, axis=1, keepdims=True), (channels, 128))
        bias[latent] = own_bias

    @pl.when(section == 0)
    def _():
        take(0)
        activate(0)

    for n in (1, 4, 5):
        loads[n].wait()
    seed = seed_ref[0]
    out_channel = lax.broadcasted_iota(jnp.int32, (8, wide), 1)
    out_part = below_mod(out_channel[0:1] * 32749)
    row_channel = lax.broadcasted_iota(jnp.int32, (channels, 128), 0) + shard * channels
    lane = lax.broadcasted_iota(jnp.int32, (channels, 128), 1)
    for tap in range(9):
        first_index = (row_channel * 9 + tap) * wide
        high = first_index >> 16
        low = high * 15 + (first_index & 65535)
        over = low >= MOD
        low = jnp.where(over, low - MOD, low)
        high = jnp.where(over, high + 1, high)
        row_part = below_mod(low * 32749 + high * 12345 + seed)
        for col in range(0, wide, 128):
            size = min(128, wide - col)
            mixed = row_part[:, :size] + out_part[:, col : col + size]
            mixed = jnp.where(low[:, :size] + lane[:, :size] >= MOD - col, mixed + 12345, mixed)
            mixed = jnp.where(mixed >= MOD, mixed - MOD, mixed)
            mixed = jnp.where(mixed >= MOD, mixed - MOD, mixed)
            noise = mixed.astype(jnp.float32) / 65521.0 - 0.5
            weight[tap * channels : (tap + 1) * channels, col : col + size] = (
                base_ref[tap, :, col : col + size].astype(jnp.float32) + 0.02 * noise
            ).astype(jnp.bfloat16)
    weight_t[...] = weight[...].T

    for s in range(sections):
        amount = replicas - 1 + shards * ((s > 0) + (s < last)) + (shards - 1) * (s == last)

        @pl.when(section == s)
        def _(amount=amount):
            pl.semaphore_wait(barrier, amount)

    @pl.when(section > 0)
    def _():
        take(0)
        send_shift(0)
        activate(0)

    @pl.when(section == 0)
    def _():
        send_shift(0)

    emit(0)
    for latent in range(1, latents_here):
        take(latent)
        send_shift(latent)
        activate(latent)
        emit(latent)

    grad_back = grad_send.at[1]
    grad_first = grad_send.at[0]

    for latent in range(latents_here):

        @pl.when(section == last)
        def _(latent=latent):
            wait_for(part_recv.at[1, latent], part_sem.at[1, latent])
            output = summed(1, latent, shift_send[latent]).astype(jnp.float32)
            grad_first[latent] = (
                (output - target_ref[latent].astype(jnp.float32)) / float(all_latents)
            ).astype(jnp.bfloat16)
            for j in order:
                peer = lax.rem(shard + j, shards)
                if j:
                    send(
                        grad_first.at[latent],
                        grad_recv.at[latent, shard],
                        send_sem.at[3, latent],
                        grad_sem.at[latent],
                        {"tensor": peer},
                    )
                else:
                    pltpu.make_async_copy(
                        grad_first.at[latent], grad_recv.at[latent, shard], grad_sem.at[latent]
                    ).start()

    for latent in range(latents_here):
        wait_for(grad_recv.at[latent], grad_sem.at[latent])
        out_grad = grad_recv[latent].reshape(wide, pixels)

        @pl.when(section > 0)
        def _(latent=latent, out_grad=out_grad):
            spread = jnp.dot(weight[...], out_grad, preferred_element_type=jnp.float32)
            col_grad = None
            for dj in (-1, 0, 1):
                down = None
                for di in (-1, 0, 1):
                    tap = (di + 1) * 3 + dj + 1
                    term = spread[tap * channels : (tap + 1) * channels]
                    if di:
                        term = moved(jnp.where(masks[di][0], term, 0.0), -di * RES)
                    down = term if down is None else down + term
                if dj:
                    down = moved(jnp.where(masks[dj][1], down, 0.0), -dj)
                col_grad = down if col_grad is None else col_grad + down
            value = normed[latent]
            inner = col_grad * slope[latent]
            mean_inner, mean_both = group_sums([inner, inner * value], GROUP)
            in_grad = scale[latent][:, 0:1] * (
                inner - mean_inner / count - value * (mean_both / count)
            )
            grad_back[latent] = (
                grad_recv[latent, shard].astype(jnp.float32) + in_grad
            ).astype(jnp.bfloat16)
            for j in order:
                send(
                    grad_back.at[latent],
                    grad_recv.at[latent, shard],
                    send_sem.at[1, latent],
                    grad_sem.at[latent],
                    {
                        "section": section - 1,
                        "tensor": lax.rem(shard + j, shards),
                    },
                )

        part = lax.dot_general(
            columns[latent], out_grad, (((1,), (1,)), ((), ())), preferred_element_type=jnp.float32
        )
        if latent == 0 and latents_here > 1:
            total[...] = part
        elif latent < latents_here - 1:
            total[...] += part
        else:
            if latent:
                part = total[...] + part
            rows = part.shape[0]
            sum_send[:rows] = part.astype(jnp.bfloat16)
            if rows < sum_send.shape[0]:
                sum_send[rows:] = jnp.zeros((sum_send.shape[0] - rows, wide), jnp.bfloat16)

    def added(ref, rows):
        result = ref[0, rows].astype(jnp.float32)
        for j in range(1, ref.shape[0]):
            result = result + ref[j, rows].astype(jnp.float32)
        return result.astype(jnp.bfloat16)

    def place_of(c, x_to, y_to, strip=False):
        start, piece = chunks[c]
        row = start + (x_to * other_side + y_to) * piece
        return pl.ds(pl.multiple_of(row, 16), piece * (other_side if strip else 1))

    def kept(c, strip=False):
        start, piece = chunks[c]
        scale_by = side if strip else replicas
        return pl.ds(start // scale_by, piece * (other_side if strip else 1))

    @pl.when(section == 0)
    def _():
        for c in range(len(chunks)):
            for j in range(1, replicas + 1):
                owner = lax.rem(dp + j, replicas)
                source = sum_send.at[place_of(c, 0, owner)]
                place = sum_recv.at[dp, kept(c)]
                if j < replicas:
                    send(source, place, send_sem.at[4, 0], sum_sem.at[c], {"dp": owner})
                else:
                    pltpu.make_async_copy(source, place, sum_sem.at[c]).start()
        for c in range(len(chunks)):
            rows = kept(c)
            wait_for(sum_recv.at[:, rows], sum_sem.at[c])
            own_sum[rows] = added(sum_recv, rows)
            place = sum_done.at[place_of(c, 0, dp)]
            for j in range(1, replicas + 1):
                if j < replicas:
                    other = {"dp": lax.rem(dp + j, replicas)}
                    send(own_sum.at[rows], place, send_sem.at[4, 1], out_sem.at[0], other)
                else:
                    pltpu.make_async_copy(own_sum.at[rows], place, out_sem.at[0]).start()
        wait_for(sum_done, out_sem.at[0])
        wait_for(sum_recv.at[pl.ds(0, replicas - 1)], send_sem.at[4, 0])
        wait_for(sum_recv.at[pl.ds(0, replicas - 1)], send_sem.at[4, 1])

    @pl.when(section > 0)
    def _():
        def along_x(c):
            for j in range(1, side + 1):
                to = lax.rem(x + j, side)
                source = sum_send.at[place_of(c, to, 0, True)]
                place = across_recv.at[x, kept(c, True)]
                if j < side:
                    device = {"dp": to * other_side + y}
                    send(source, place, send_sem.at[4, 0], sum_sem.at[c], device)
                else:
                    pltpu.make_async_copy(source, place, sum_sem.at[c]).start()

        def along_y(c):
            start, piece = chunks[c]
            rows = kept(c, True)
            wait_for(across_recv.at[:, rows], sum_sem.at[c])
            across_sum[rows] = added(across_recv, rows)
            for j in range(1, other_side + 1):
                to = lax.rem(y + j, other_side)
                row = pl.multiple_of(start // side + to * piece, 16)
                source = across_sum.at[pl.ds(row, piece)]
                place = sum_recv.at[y, kept(c)]
                if j < other_side:
                    device = {"dp": x * other_side + to}
                    send(source, place, send_sem.at[4, 1], down_sem.at[c], device)
                else:
                    pltpu.make_async_copy(source, place, down_sem.at[c]).start()

        def back_y(c):
            rows = kept(c)
            wait_for(sum_recv.at[pl.ds(0, other_side), rows], down_sem.at[c])
            own_sum[rows] = added(sum_recv.at[pl.ds(0, other_side)], rows)
            place = sum_done.at[place_of(c, x, y)]
            for j in range(1, other_side + 1):
                if j < other_side:
                    device = {"dp": x * other_side + lax.rem(y + j, other_side)}
                    send(own_sum.at[rows], place, send_sem.at[5, 0], up_sem.at[c], device)
                else:
                    pltpu.make_async_copy(own_sum.at[rows], place, up_sem.at[c]).start()

        def back_x(c):
            mine = sum_done.at[place_of(c, x, 0, True)]
            wait_for(mine, up_sem.at[c])
            for j in range(1, side):
                device = {"dp": lax.rem(x + j, side) * other_side + y}
                send(mine, mine, send_sem.at[5, 1], out_sem.at[0], device)

        for c in range(len(chunks)):
            along_x(c)
        stages = (along_y, back_y, back_x)
        for step in range(len(chunks) + len(stages) - 1):
            for n in reversed(range(len(stages))):
                if 0 <= step - n < len(chunks):
                    stages[n](step - n)
        others = across_recv.at[pl.ds(0, side - 1)]
        wait_for(others, out_sem.at[0])
        wait_for(others, send_sem.at[4, 0])
        wait_for(others, send_sem.at[5, 1])
        for n in ((4, 1), (5, 0)):
            wait_for(sum_recv.at[pl.ds(0, other_side - 1)], send_sem.at[n])

    result = pltpu.make_async_copy(sum_done.at[pl.ds(0, out_ref.shape[0])], out_ref, out_sem.at[1])
    result.start()

    for latent in range(latents_here):

        @pl.when(section < last)
        def _(latent=latent):
            wait_for(part_send.at[latent], send_sem.at[0, latent])
            wait_for(shift_send.at[latent], send_sem.at[2, latent])

        @pl.when(section == last)
        def _(latent=latent):
            others = part_send.at[latent, pl.ds(0, shards - 1)]
            wait_for(others, send_sem.at[0, latent])
            wait_for(others, send_sem.at[3, latent])

        @pl.when(section > 0)
        def _(latent=latent):
            wait_for(part_send.at[latent], send_sem.at[1, latent])

    result.wait()


def body(latents, target, base_weight, seeds, timesteps, time_table):
    replicas, sections, shards = (lax.axis_size(name) for name in ("dp", "section", "tensor"))
    channels, latents_here, pixels = latents.shape
    wide = base_weight.shape[3]
    rows = 9 * channels
    piece = sum(PIECES)
    side = min(SIDE, replicas)
    strip = piece * (replicas // side)
    sizes = (replicas, sections, shards, latents_here, latents_here * replicas)
    hbm = pl.BlockSpec(memory_space=pltpu.HBM)
    bf16, f32 = jnp.bfloat16, jnp.float32
    here = latents_here
    scratch = [
        pltpu.VMEM((here, channels, pixels), bf16),
        pltpu.VMEM((here, channels, pixels), bf16),
        pltpu.VMEM((9, channels, wide), bf16),
        pltpu.VMEM(time_table.shape[:0:-1], bf16),
        pltpu.SMEM((1,), jnp.int32),
        pltpu.SMEM((here,), jnp.int32),
        pltpu.SemaphoreType.DMA((6,)),
        pltpu.VMEM((rows, wide), bf16),
        pltpu.VMEM((wide, rows), bf16),
        pltpu.VMEM((here, channels, 128), f32),
        pltpu.VMEM((here, shards, channels, pixels), bf16),
        pltpu.VMEM((2, here, shards, channels, pixels), bf16),
        pltpu.VMEM((here, channels, pixels), f32),
        pltpu.VMEM((here, channels, pixels), f32),
        pltpu.VMEM((2, here, channels, pixels), bf16),
        pltpu.VMEM((here, shards, channels, pixels), bf16),
        pltpu.VMEM((here, rows, pixels), bf16),
        pltpu.VMEM((here, channels, pixels), f32),
        pltpu.VMEM((here, channels, 128), f32),
        pltpu.VMEM((here, channels, pixels), f32),
        pltpu.VMEM((channels, pixels), f32),
        pltpu.VMEM((rows, wide), f32),
        pltpu.VMEM((replicas * piece, wide), bf16),
        pltpu.VMEM((replicas, piece, wide), bf16),
        pltpu.VMEM((piece, wide), bf16),
        pltpu.VMEM((side, strip, wide), bf16),
        pltpu.VMEM((strip, wide), bf16),
        pltpu.VMEM((replicas * piece, wide), bf16),
        pltpu.SemaphoreType.DMA((len(PIECES),)),
        pltpu.SemaphoreType.DMA((len(PIECES),)),
        pltpu.SemaphoreType.DMA((2, here)),
        pltpu.SemaphoreType.DMA((here,)),
        pltpu.SemaphoreType.DMA((here,)),
        pltpu.SemaphoreType.DMA((len(PIECES),)),
        pltpu.SemaphoreType.DMA((2,)),
        pltpu.SemaphoreType.DMA((6, 2)),
    ]
    result = pl.pallas_call(
        functools.partial(kernel, sizes),
        out_shape=jax.ShapeDtypeStruct((rows, wide), bf16),
        in_specs=[hbm] * 6,
        out_specs=hbm,
        scratch_shapes=scratch,
        compiler_params=pltpu.CompilerParams(
            collective_id=0, has_side_effects=True, vmem_limit_bytes=63 * 1024 * 1024
        ),
        cost_estimate=pl.CostEstimate(
            flops=6 * here * rows * wide * pixels, bytes_accessed=4 * rows * wide, transcendentals=0
        ),
    )(
        latents.transpose(1, 0, 2),
        target.transpose(1, 0, 2),
        base_weight[0].transpose(1, 0, 2),
        seeds,
        timesteps,
        time_table[0].T,
    )
    return result.astype(f32).reshape(9, channels, wide).transpose(1, 0, 2)[None]


def solution(mesh):
    in_specs = (
        P("tensor", "dp", None),
        P("tensor", "dp", None),
        P("section", "tensor", None, None),
        P("section"),
        P("dp"),
        P("section", None, "tensor"),
    )
    out_specs = P("section", "tensor", None, None)
    return jax.shard_map(body, mesh=mesh, in_specs=in_specs, out_specs=out_specs, check_vma=False)
```

time: 118 us -> 116 us (0.983); the launches traced: 118 us -> 115 us
  local copies, waits for them, and re-layouts: 3.77 us -> 1.61 us
  Pallas kernels: 112 us -> 110 us
    unnamed x6 -> x0, local copies, waits for them, and re-layouts: 2.75 us -> none
    pallas_call x1, Pallas kernels: 112 us -> 110 us  [body(): pl.pallas_call(functools.partial(kernel, sizes), out_shape=jax.ShapeDtype...]
where the time goes in v3:
time: 116 us; the launch traced here: 115 us
  Pallas kernels  110 us (95%)
  other arithmetic  2.53 us (2%)
  local copies, waits for them, and re-layouts  1.61 us (1%)
    pallas_call x1, Pallas kernels, body(): pl.pallas_call(functools.partial(kernel, sizes), out_shape=jax.ShapeDtype...  110 us
    broadcast_in_dim x1, other arithmetic, body(): result.astype(f32).reshape(9, channels, wide).transpose(1, 0, 2)[None]  2.53 us

profile of v3, /device:TPU:1, one launch (start us, length us, event | category | flops | bytes accessed | tf_op | source)
XLA Modules:
  0.0 114.6 jit_solution(12183919936163629395)
XLA Ops:
  0.7 1.6 %copy_bitcast_fusion = (bf16[2,80,256]{2,1,0:T(8,128)(2,1)}, bf16[2,80,256]{2,1,0:T(8,128)(2,1)}) fusion(bf16[80,2,256]{2,1,0:T(2,128)(2,1)} %param.7, bf16[80,2,256]{2,1,0:T(2,128)(2,1)} %param.6), kind=kLoop, calls=%fused_computation.1 | loop fusion | bytes 327680 | tf_op jit(solution)/shard_map/transpose | solution.py:625
  2.3 109.8 %shard_map.64 = bf16[720,640]{1,0:T(8,128)(2,1)} custom-call(bf16[2,80,256]{2,1,0:T(8,128)(2,1)} %get-tuple-element.6.latents_hbm, bf16[2,80,256]{2,1,0:T(8,128)(2,1)} %get-tuple-element.5.target_hbm, bf16[9,80,640]{2,1,0:T(8,128)(2,1)} %bitcast.17, s32[1]{0:T(128)S(6)} %copy.11.seed_hbm, s32[2]{0:T(128)} %steps_hbm.1, bf16[80,1000]{1,0:T(8,128)(2,1)} %bitcast.18), custom_call_target="tpu_custom_call" | custom-call | flops 1415577600 | bytes 1843200 | tf_op jit(solution)/shard_map/pallas_call | solution.py:611
  112.1 2.5 %convert_bitcast_fusion = f32[1,80,9,640]{3,1,2,0:T(8,128)} fusion(bf16[9,80,640]{2,1,0:T(8,128)(2,1)} %bitcast.16), kind=kLoop, calls=%fused_computation | loop fusion | flops 460800 | bytes 2764800 | tf_op jit(solution)/shard_map/broadcast_in_dim | solution.py:631

commit v4 on v3

--- a/solution.py
+++ b/solution.py
@@ -188,11 +188,18 @@
     order = [j for j in (4, 3, 5, 2, 6, 1, 7, 0) if j < shards]
     order += [j for j in range(shards) if j not in order]
 
+    def make_part(latent, peer):
+        rows = pl.ds(pl.multiple_of(peer * channels, 16), channels)
+        part_send[latent, peer] = jnp.dot(
+            weight_t[rows], columns[latent], preferred_element_type=jnp.float32
+        ).astype(jnp.bfloat16)
+
     def send_parts(latent):
         @pl.when(section < last)
         def _():
             for j in order:
                 peer = lax.rem(shard + j, shards)
+                make_part(latent, peer)
                 send(
                     part_send.at[latent, peer],
                     part_recv.at[0, latent, shard],
@@ -205,6 +212,7 @@
         def _():
             for j in order:
                 peer = lax.rem(shard + j, shards)
+                make_part(latent, peer)
                 if j:
                     send(
                         part_send.at[latent, peer],
@@ -274,11 +282,6 @@
         scale[latent] = jnp.broadcast_to(factor, (channels, 128))
 
     def emit(latent):
-        part_send[latent] = (
-            jnp.dot(weight_t[...], columns[latent], preferred_element_type=jnp.float32)
-            .astype(jnp.bfloat16)
-            .reshape(shards, channels, pixels)
-        )
         send_parts(latent)
         sigmoid = slope[latent]
         slope[latent] = sigmoid * (1.0 + normed[latent] * (1.0 - sigmoid))
@@ -447,14 +450,22 @@
         scale_by = side if strip else replicas
         return pl.ds(start // scale_by, piece * (other_side if strip else 1))
 
+    def around(size):
+        return sorted(range(size), key=lambda j: -min(j, size - j))
+
+    steps = [(i, j) for i in range(side) for j in range(other_side)]
+    steps.sort(key=lambda ij: -min(ij[0], side - ij[0]) - 2 * min(ij[1], other_side - ij[1]))
+    far_first = [
+        (i + j, lax.rem(x + i, side) * other_side + lax.rem(y + j, other_side)) for i, j in steps
+    ]
+
     @pl.when(section == 0)
     def _():
         for c in range(len(chunks)):
-            for j in range(1, replicas + 1):
-                owner = lax.rem(dp + j, replicas)
+            for j, owner in far_first:
                 source = sum_send.at[place_of(c, 0, owner)]
                 place = sum_recv.at[dp, kept(c)]
-                if j < replicas:
+                if j:
                     send(source, place, send_sem.at[4, 0], sum_sem.at[c], {"dp": owner})
                 else:
                     pltpu.make_async_copy(source, place, sum_sem.at[c]).start()
@@ -463,10 +474,11 @@
             wait_for(sum_recv.at[:, rows], sum_sem.at[c])
             own_sum[rows] = added(sum_recv, rows)
             place = sum_done.at[place_of(c, 0, dp)]
-            for j in range(1, replicas + 1):
-                if j < replicas:
-                    other = {"dp": lax.rem(dp + j, replicas)}
-                    send(own_sum.at[rows], place, send_sem.at[4, 1], out_sem.at[0], other)
+            for j, other in far_first:
+                if j:
+                    send(
+                        own_sum.at[rows], place, send_sem.at[4, 1], out_sem.at[0], {"dp": other}
+                    )
                 else:
                     pltpu.make_async_copy(own_sum.at[rows], place, out_sem.at[0]).start()
         wait_for(sum_done, out_sem.at[0])
@@ -476,11 +488,11 @@
     @pl.when(section > 0)
     def _():
         def along_x(c):
-            for j in range(1, side + 1):
+            for j in around(side):
                 to = lax.rem(x + j, side)
                 source = sum_send.at[place_of(c, to, 0, True)]
                 place = across_recv.at[x, kept(c, True)]
-                if j < side:
+                if j:
                     device = {"dp": to * other_side + y}
                     send(source, place, send_sem.at[4, 0], sum_sem.at[c], device)
                 else:
@@ -491,12 +503,12 @@
             rows = kept(c, True)
             wait_for(across_recv.at[:, rows], sum_sem.at[c])
             across_sum[rows] = added(across_recv, rows)
-            for j in range(1, other_side + 1):
+            for j in around(other_side):
                 to = lax.rem(y + j, other_side)
                 row = pl.multiple_of(start // side + to * piece, 16)
                 source = across_sum.at[pl.ds(row, piece)]
                 place = sum_recv.at[y, kept(c)]
-                if j < other_side:
+                if j:
                     device = {"dp": x * other_side + to}
                     send(source, place, send_sem.at[4, 1], down_sem.at[c], device)
                 else:
@@ -507,8 +519,8 @@
             wait_for(sum_recv.at[pl.ds(0, other_side), rows], down_sem.at[c])
             own_sum[rows] = added(sum_recv.at[pl.ds(0, other_side)], rows)
             place = sum_done.at[place_of(c, x, y)]
-            for j in range(1, other_side + 1):
-                if j < other_side:
+            for j in around(other_side):
+                if j:
                     device = {"dp": x * other_side + lax.rem(y + j, other_side)}
                     send(own_sum.at[rows], place, send_sem.at[5, 0], up_sem.at[c], device)
                 else:
@@ -517,7 +529,7 @@
         def back_x(c):
             mine = sum_done.at[place_of(c, x, 0, True)]
             wait_for(mine, up_sem.at[c])
-            for j in range(1, side):
+            for j in around(side)[:-1]:
                 device = {"dp": lax.rem(x + j, side) * other_side + y}
                 send(mine, mine, send_sem.at[5, 1], out_sem.at[0], device)
 

time: 116 us -> 114 us (0.983)
  Pallas kernels: 110 us -> 108 us
    pallas_call x1, Pallas kernels: 110 us -> 108 us  [body(): pl.pallas_call(functools.partial(kernel, sizes), out_shape=jax.ShapeDtype...]
where the time goes in v4:
time: 114 us; the launch traced here: 113 us
  Pallas kernels  108 us (95%)
  other arithmetic  2.53 us (2%)
  local copies, waits for them, and re-layouts  1.61 us (1%)
    pallas_call x1, Pallas kernels, body(): pl.pallas_call(functools.partial(kernel, sizes), out_shape=jax.ShapeDtype...  108 us
    broadcast_in_dim x1, other arithmetic, body(): result.astype(f32).reshape(9, channels, wide).transpose(1, 0, 2)[None]  2.53 us

profile of v4, /device:TPU:1, one launch (start us, length us, event | category | flops | bytes accessed | tf_op | source)
XLA Modules:
  0.0 113.3 jit_solution(15474077712793438987)
XLA Ops:
  0.7 1.6 %copy_bitcast_fusion = (bf16[2,80,256]{2,1,0:T(8,128)(2,1)}, bf16[2,80,256]{2,1,0:T(8,128)(2,1)}) fusion(bf16[80,2,256]{2,1,0:T(2,128)(2,1)} %param.7, bf16[80,2,256]{2,1,0:T(2,128)(2,1)} %param.6), kind=kLoop, calls=%fused_computation.1 | loop fusion | bytes 327680 | tf_op jit(solution)/shard_map/transpose | solution.py:637
  2.3 108.5 %shard_map.64 = bf16[720,640]{1,0:T(8,128)(2,1)} custom-call(bf16[2,80,256]{2,1,0:T(8,128)(2,1)} %get-tuple-element.6.latents_hbm, bf16[2,80,256]{2,1,0:T(8,128)(2,1)} %get-tuple-element.5.target_hbm, bf16[9,80,640]{2,1,0:T(8,128)(2,1)} %bitcast.17, s32[1]{0:T(128)S(6)} %copy.11.seed_hbm, s32[2]{0:T(128)} %steps_hbm.1, bf16[80,1000]{1,0:T(8,128)(2,1)} %bitcast.18), custom_call_target="tpu_custom_call" | custom-call | flops 1415577600 | bytes 1843200 | tf_op jit(solution)/shard_map/pallas_call | solution.py:623
  110.8 2.5 %convert_bitcast_fusion = f32[1,80,9,640]{3,1,2,0:T(8,128)} fusion(bf16[9,80,640]{2,1,0:T(8,128)(2,1)} %bitcast.16), kind=kLoop, calls=%fused_computation | loop fusion | flops 460800 | bytes 2764800 | tf_op jit(solution)/shard_map/broadcast_in_dim | solution.py:643

commit v5 on v4

--- a/solution.py
+++ b/solution.py
@@ -237,7 +237,7 @@
     def take(latent):
         @pl.when(section == 0)
         def _():
-            held[...] = latents_ref[latent].astype(jnp.float32)
+            held[...] = latents_ref[...].astype(jnp.float32)[:, latent]
 
         @pl.when(section > 0)
         def _():
@@ -362,7 +362,7 @@
             wait_for(part_recv.at[1, latent], part_sem.at[1, latent])
             output = summed(1, latent, shift_send[latent]).astype(jnp.float32)
             grad_first[latent] = (
-                (output - target_ref[latent].astype(jnp.float32)) / float(all_latents)
+                (output - target_ref[...].astype(jnp.float32)[:, latent]) / float(all_latents)
             ).astype(jnp.bfloat16)
             for j in order:
                 peer = lax.rem(shard + j, shards)
@@ -378,6 +378,61 @@
                     pltpu.make_async_copy(
                         grad_first.at[latent], grad_recv.at[latent, shard], grad_sem.at[latent]
                     ).start()
+
+    def added(ref, rows):
+        result = ref[0, rows].astype(jnp.float32)
+        for j in range(1, ref.shape[0]):
+            result = result + ref[j, rows].astype(jnp.float32)
+        return result.astype(jnp.bfloat16)
+
+    def place_of(c, x_to, y_to, strip=False):
+        start, piece = chunks[c]
+        row = start + (x_to * other_side + y_to) * piece
+        return pl.ds(pl.multiple_of(row, 16), piece * (other_side if strip else 1))
+
+    def kept(c, strip=False):
+        start, piece = chunks[c]
+        scale_by = side if strip else replicas
+        return pl.ds(start // scale_by, piece * (other_side if strip else 1))
+
+    def around(size):
+        return sorted(range(size), key=lambda j: -min(j, size - j))
+
+    steps = [(i, j) for i in range(side) for j in range(other_side)]
+    steps.sort(key=lambda ij: -min(ij[0], side - ij[0]) - 2 * min(ij[1], other_side - ij[1]))
+    far_first = [
+        (i + j, lax.rem(x + i, side) * other_side + lax.rem(y + j, other_side)) for i, j in steps
+    ]
+
+    def along_x(c):
+        for j in around(side):
+            to = lax.rem(x + j, side)
+            source = sum_send.at[place_of(c, to, 0, True)]
+            place = across_recv.at[x, kept(c, True)]
+            if j:
+                device = {"dp": to * other_side + y}
+                send(source, place, send_sem.at[4, 0], sum_sem.at[c], device)
+            else:
+                pltpu.make_async_copy(source, place, sum_sem.at[c]).start()
+
+    def along_y(c):
+        start, piece = chunks[c]
+        rows = kept(c, True)
+        wait_for(across_recv.at[:, rows], sum_sem.at[c])
+        across_sum[rows] = added(across_recv, rows)
+        for j in around(other_side):
+            to = lax.rem(y + j, other_side)
+            row = pl.multiple_of(start // side + to * piece, 16)
+            source = across_sum.at[pl.ds(row, piece)]
+            place = sum_recv.at[y, kept(c)]
+            if j:
+                device = {"dp": x * other_side + to}
+                send(source, place, send_sem.at[4, 1], down_sem.at[c], device)
+            else:
+                pltpu.make_async_copy(source, place, down_sem.at[c]).start()
+
+    padding = sum_send.shape[0] - weight.shape[0]
+    sum_send[pl.ds(weight.shape[0], padding)] = jnp.zeros((padding, wide), jnp.bfloat16)
 
     for latent in range(latents_here):
         wait_for(grad_recv.at[latent], grad_sem.at[latent])
@@ -419,101 +474,45 @@
                     },
                 )
 
-        part = lax.dot_general(
-            columns[latent], out_grad, (((1,), (1,)), ((), ())), preferred_element_type=jnp.float32
-        )
-        if latent == 0 and latents_here > 1:
-            total[...] = part
-        elif latent < latents_here - 1:
-            total[...] += part
-        else:
+        for c, (start, piece) in enumerate(chunks):
+            rows = pl.ds(start, min(piece * replicas, weight.shape[0] - start))
+            part = lax.dot_general(
+                columns[latent, rows],
+                out_grad,
+                (((1,), (1,)), ((), ())),
+                preferred_element_type=jnp.float32,
+            )
             if latent:
-                part = total[...] + part
-            rows = part.shape[0]
-            sum_send[:rows] = part.astype(jnp.bfloat16)
-            if rows < sum_send.shape[0]:
-                sum_send[rows:] = jnp.zeros((sum_send.shape[0] - rows, wide), jnp.bfloat16)
-
-    def added(ref, rows):
-        result = ref[0, rows].astype(jnp.float32)
-        for j in range(1, ref.shape[0]):
-            result = result + ref[j, rows].astype(jnp.float32)
-        return result.astype(jnp.bfloat16)
-
-    def place_of(c, x_to, y_to, strip=False):
-        start, piece = chunks[c]
-        row = start + (x_to * other_side + y_to) * piece
-        return pl.ds(pl.multiple_of(row, 16), piece * (other_side if strip else 1))
-
-    def kept(c, strip=False):
-        start, piece = chunks[c]
-        scale_by = side if strip else replicas
-        return pl.ds(start // scale_by, piece * (other_side if strip else 1))
-
-    def around(size):
-        return sorted(range(size), key=lambda j: -min(j, size - j))
-
-    steps = [(i, j) for i in range(side) for j in range(other_side)]
-    steps.sort(key=lambda ij: -min(ij[0], side - ij[0]) - 2 * min(ij[1], other_side - ij[1]))
-    far_first = [
-        (i + j, lax.rem(x + i, side) * other_side + lax.rem(y + j, other_side)) for i, j in steps
-    ]
+                part = total[rows] + part
+            if latent < latents_here - 1:
+                total[rows] = part
+            else:
+                sum_send[rows] = part.astype(jnp.bfloat16)
+                along_x(c)
 
     @pl.when(section == 0)
     def _():
         for c in range(len(chunks)):
-            for j, owner in far_first:
-                source = sum_send.at[place_of(c, 0, owner)]
-                place = sum_recv.at[dp, kept(c)]
-                if j:
-                    send(source, place, send_sem.at[4, 0], sum_sem.at[c], {"dp": owner})
-                else:
-                    pltpu.make_async_copy(source, place, sum_sem.at[c]).start()
+            along_y(c)
         for c in range(len(chunks)):
             rows = kept(c)
-            wait_for(sum_recv.at[:, rows], sum_sem.at[c])
-            own_sum[rows] = added(sum_recv, rows)
+            wait_for(sum_recv.at[pl.ds(0, other_side), rows], down_sem.at[c])
+            own_sum[rows] = added(sum_recv.at[pl.ds(0, other_side)], rows)
             place = sum_done.at[place_of(c, 0, dp)]
             for j, other in far_first:
                 if j:
                     send(
-                        own_sum.at[rows], place, send_sem.at[4, 1], out_sem.at[0], {"dp": other}
+                        own_sum.at[rows], place, send_sem.at[5, 0], out_sem.at[0], {"dp": other}
                     )
                 else:
                     pltpu.make_async_copy(own_sum.at[rows], place, out_sem.at[0]).start()
         wait_for(sum_done, out_sem.at[0])
-        wait_for(sum_recv.at[pl.ds(0, replicas - 1)], send_sem.at[4, 0])
-        wait_for(sum_recv.at[pl.ds(0, replicas - 1)], send_sem.at[4, 1])
+        wait_for(across_recv.at[pl.ds(0, side - 1)], send_sem.at[4, 0])
+        wait_for(sum_recv.at[pl.ds(0, other_side - 1)], send_sem.at[4, 1])
+        wait_for(sum_recv.at[pl.ds(0, replicas - 1)], send_sem.at[5, 0])
 
     @pl.when(section > 0)
     def _():
-        def along_x(c):
-            for j in around(side):
-                to = lax.rem(x + j, side)
-                source = sum_send.at[place_of(c, to, 0, True)]
-                place = across_recv.at[x, kept(c, True)]
-                if j:
-                    device = {"dp": to * other_side + y}
-                    send(source, place, send_sem.at[4, 0], sum_sem.at[c], device)
-                else:
-                    pltpu.make_async_copy(source, place, sum_sem.at[c]).start()
-
-        def along_y(c):
-            start, piece = chunks[c]
-            rows = kept(c, True)
-            wait_for(across_recv.at[:, rows], sum_sem.at[c])
-            across_sum[rows] = added(across_recv, rows)
-            for j in around(other_side):
-                to = lax.rem(y + j, other_side)
-                row = pl.multiple_of(start // side + to * piece, 16)
-                source = across_sum.at[pl.ds(row, piece)]
-                place = sum_recv.at[y, kept(c)]
-                if j:
-                    device = {"dp": x * other_side + to}
-                    send(source, place, send_sem.at[4, 1], down_sem.at[c], device)
-                else:
-                    pltpu.make_async_copy(source, place, down_sem.at[c]).start()
-
         def back_y(c):
             rows = kept(c)
             wait_for(sum_recv.at[pl.ds(0, other_side), rows], down_sem.at[c])
@@ -533,8 +532,6 @@
                 device = {"dp": lax.rem(x + j, side) * other_side + y}
                 send(mine, mine, send_sem.at[5, 1], out_sem.at[0], device)
 
-        for c in range(len(chunks)):
-            along_x(c)
         stages = (along_y, back_y, back_x)
         for step in range(len(chunks) + len(stages) - 1):
             for n in reversed(range(len(stages))):
@@ -583,8 +580,8 @@
     bf16, f32 = jnp.bfloat16, jnp.float32
     here = latents_here
     scratch = [
-        pltpu.VMEM((here, channels, pixels), bf16),
-        pltpu.VMEM((here, channels, pixels), bf16),
+        pltpu.VMEM((channels, here, pixels), bf16),
+        pltpu.VMEM((channels, here, pixels), bf16),
         pltpu.VMEM((9, channels, wide), bf16),
         pltpu.VMEM(time_table.shape[:0:-1], bf16),
         pltpu.SMEM((1,), jnp.int32),
@@ -633,8 +630,8 @@
             flops=6 * here * rows * wide * pixels, bytes_accessed=4 * rows * wide, transcendentals=0
         ),
     )(
-        latents.transpose(1, 0, 2),
-        target.transpose(1, 0, 2),
+        latents,
+        target,
         base_weight[0].transpose(1, 0, 2),
         seeds,
         timesteps,

time: 114 us -> 112 us (0.982)
  local copies, waits for them, and re-layouts: 1.61 us -> 0 us
    transpose x1 -> x0, local copies, waits for them, and re-layouts: 1.61 us -> none  [body(): target.transpose(1, 0, 2)]
    pallas_call x1, Pallas kernels: 108 us -> 107 us  [body(): pl.pallas_call(functools.partial(kernel, sizes), out_shape=jax.ShapeDtype...]
where the time goes in v5:
time: 112 us; the launch traced here: 110 us
  Pallas kernels  107 us (96%)
  other arithmetic  2.53 us (2%)
    pallas_call x1, Pallas kernels, body(): pl.pallas_call(functools.partial(kernel, sizes), out_shape=jax.ShapeDtype...  107 us
    broadcast_in_dim x1, other arithmetic, body(): result.astype(f32).reshape(9, channels, wide).transpose(1, 0, 2)[None]  2.53 us

profile of v5, /device:TPU:1, one launch (start us, length us, event | category | flops | bytes accessed | tf_op | source)
XLA Modules:
  0.0 110.3 jit_solution(5622393220715650412)
XLA Ops:
  0.7 107.1 %shard_map.64 = bf16[720,640]{1,0:T(8,128)(2,1)} custom-call(bf16[80,2,256]{2,1,0:T(2,128)(2,1)} %latents_hbm.1, bf16[80,2,256]{2,1,0:T(2,128)(2,1)} %target_hbm.1, bf16[9,80,640]{2,1,0:T(8,128)(2,1)} %bitcast.13, s32[1]{0:T(128)S(6)} %copy.7.seed_hbm, s32[2]{0:T(128)} %steps_hbm.1, bf16[80,1000]{1,0:T(8,128)(2,1)} %bitcast.14), custom_call_target="tpu_custom_call" | custom-call | flops 1415577600 | bytes 1843200 | tf_op jit(solution)/shard_map/pallas_call | solution.py:620
  107.7 2.5 %convert_bitcast_fusion = f32[1,80,9,640]{3,1,2,0:T(8,128)} fusion(bf16[9,80,640]{2,1,0:T(8,128)(2,1)} %bitcast.12), kind=kLoop, calls=%fused_computation | loop fusion | flops 460800 | bytes 2764800 | tf_op jit(solution)/shard_map/broadcast_in_dim | solution.py:640

commit v6 on v5

--- a/solution.py
+++ b/solution.py
@@ -108,6 +108,9 @@
     sum_sem,
     out_sem,
     send_sem,
+    input_send,
+    bias_before,
+    bias_sem,
 ):
     replicas, sections, shards, latents_here, all_latents = sizes
     dp = lax.axis_index("dp")
@@ -241,17 +244,21 @@
 
         @pl.when(section > 0)
         def _():
+            if latent == 0:
+                wait_for(bias_before, bias_sem.at[1])
             wait_for(shift_recv.at[latent], shift_sem.at[latent])
             wait_for(part_recv.at[0, latent], part_sem.at[0, latent])
-            held[...] = summed(0, latent, shift_recv[latent]).astype(jnp.float32)
-
+            start = shift_recv[latent].astype(jnp.float32) + bias_before[latent][:, 0:1]
+            held[...] = summed(0, latent, start).astype(jnp.float32)
+
+        input_send[latent] = held[...].astype(jnp.bfloat16)
         shift_send[latent] = held[...] + bias[latent][:, 0:1]
 
     def send_shift(latent):
         @pl.when(section < last)
         def _():
             send(
-                shift_send.at[latent],
+                input_send.at[latent],
                 shift_recv.at[latent],
                 send_sem.at[2, latent],
                 shift_sem.at[latent],
@@ -334,6 +341,10 @@
         @pl.when(section == s)
         def _(amount=amount):
             pl.semaphore_wait(barrier, amount)
+
+    @pl.when(section < last)
+    def _():
+        send(bias, bias_before, bias_sem.at[0], bias_sem.at[1], {"section": section + 1})
 
     @pl.when(section > 0)
     def _():
@@ -547,12 +558,16 @@
     result = pltpu.make_async_copy(sum_done.at[pl.ds(0, out_ref.shape[0])], out_ref, out_sem.at[1])
     result.start()
 
+    @pl.when(section < last)
+    def _():
+        wait_for(bias, bias_sem.at[0])
+
     for latent in range(latents_here):
 
         @pl.when(section < last)
         def _(latent=latent):
             wait_for(part_send.at[latent], send_sem.at[0, latent])
-            wait_for(shift_send.at[latent], send_sem.at[2, latent])
+            wait_for(input_send.at[latent], send_sem.at[2, latent])
 
         @pl.when(section == last)
         def _(latent=latent):
@@ -593,7 +608,7 @@
         pltpu.VMEM((here, shards, channels, pixels), bf16),
         pltpu.VMEM((2, here, shards, channels, pixels), bf16),
         pltpu.VMEM((here, channels, pixels), f32),
-        pltpu.VMEM((here, channels, pixels), f32),
+        pltpu.VMEM((here, channels, pixels), bf16),
         pltpu.VMEM((2, here, channels, pixels), bf16),
         pltpu.VMEM((here, shards, channels, pixels), bf16),
         pltpu.VMEM((here, rows, pixels), bf16),
@@ -616,6 +631,9 @@
         pltpu.SemaphoreType.DMA((len(PIECES),)),
         pltpu.SemaphoreType.DMA((2,)),
         pltpu.SemaphoreType.DMA((6, 2)),
+        pltpu.VMEM((here, channels, pixels), bf16),
+        pltpu.VMEM((here, channels, 128), f32),
+        pltpu.SemaphoreType.DMA((2,)),
     ]
     result = pl.pallas_call(
         functools.partial(kernel, sizes),

time: 112 us -> 111 us (level)
    pallas_call x1, Pallas kernels: 107 us -> 106 us  [body(): pl.pallas_call(functools.partial(kernel, sizes), out_shape=jax.ShapeDtype...]
where the time goes in v6:
time: 111 us; the launch traced here: 109 us
  Pallas kernels  106 us (95%)
  other arithmetic  2.53 us (2%)
    pallas_call x1, Pallas kernels, body(): pl.pallas_call(functools.partial(kernel, sizes), out_shape=jax.ShapeDtype...  106 us
    broadcast_in_dim x1, other arithmetic, body(): result.astype(f32).reshape(9, channels, wide).transpose(1, 0, 2)[None]  2.53 us

profile of v6, /device:TPU:1, one launch (start us, length us, event | category | flops | bytes accessed | tf_op | source)
XLA Modules:
  0.0 108.9 jit_solution(7272973924621512156)
XLA Ops:
  0.7 105.7 %shard_map.64 = bf16[720,640]{1,0:T(8,128)(2,1)} custom-call(bf16[80,2,256]{2,1,0:T(2,128)(2,1)} %latents_hbm.1, bf16[80,2,256]{2,1,0:T(2,128)(2,1)} %target_hbm.1, bf16[9,80,640]{2,1,0:T(8,128)(2,1)} %bitcast.13, s32[1]{0:T(128)S(6)} %copy.7.seed_hbm, s32[2]{0:T(128)} %steps_hbm.1, bf16[80,1000]{1,0:T(8,128)(2,1)} %bitcast.14), custom_call_target="tpu_custom_call" | custom-call | flops 1415577600 | bytes 1843200 | tf_op jit(solution)/shard_map/pallas_call | solution.py:638
  106.4 2.5 %convert_bitcast_fusion = f32[1,80,9,640]{3,1,2,0:T(8,128)} fusion(bf16[9,80,640]{2,1,0:T(8,128)(2,1)} %bitcast.12), kind=kLoop, calls=%fused_computation | loop fusion | flops 460800 | bytes 2764800 | tf_op jit(solution)/shard_map/broadcast_in_dim | solution.py:658
